TPU v7x, 256 devices: a whole 4x4x8 slice. The times are simulated.
256 devices in a mesh: replica: 32 (over x_hi, z, core), tensor: 8 (over x_lo, y).
Axes of the slice: x: 4 (x_hi: 2, x_lo: 2; x = x_hi * 2 + x_lo), y: 4, z: 8, core: 2. Of those that a mesh axis runs over, the one named last changes fastest.
Arguments:
- hidden: bfloat16 [32768, 9728], P('replica', 'tensor'), may hold values from -6 to 6
- out_grad: bfloat16 [32768, 1792], P('replica', 'tensor'), may hold values from -0.26367188 to 0.26367188
- token_mask: int32 [32768], P('replica'), may hold values 0 or 1
- momentum: bfloat16 [32, 9728, 1792], P('replica', 'tensor'), may hold values from -6 to 6
Outputs:
- momentum_out: bfloat16 [32, 9728, 1792], P('replica', 'tensor')
- band_update: bfloat16 [9728, 1792], P('tensor')
All inputs are finite; a program needn't handle non-finite values. No bound on the sum of `token_mask` on one device may be relied on, other than what follows from the above.
Results may differ from a plain program's by a relative error of at most 0.001.
Values may be sent and summed in bfloat16 or wider, within the bound.
No kernel may reach another device: no remote copies, remote signals or barrier semaphores. Data moves between devices by JAX's collectives and lax.ppermute only.
A program may use at most 128 MiB of HBM per device.

v0:
```python
import jax
import jax.numpy as jnp
from jax import lax
from jax.sharding import PartitionSpec as P

TILE = 64
BAND = 8


decay_rate = 0.9


def make_basis():
    freqs = jnp.arange(BAND, dtype=jnp.float32)
    cells = jnp.arange(TILE, dtype=jnp.float32)
    scales = jnp.where(freqs == 0, jnp.sqrt(1.0 / TILE), jnp.sqrt(2.0 / TILE)).astype(jnp.float32)
    return scales[:, None] * jnp.cos(
        jnp.pi * (2.0 * cells[None, :] + 1.0) * freqs[:, None] / (2.0 * TILE)
    )


def band_of(source, dct_basis):
    row_count, col_count = source.shape
    tiled = source.reshape(row_count // TILE, TILE, col_count)
    row_pass = jnp.einsum("ai,xiz->xaz", dct_basis, tiled, precision=lax.Precision.HIGHEST)
    row_pass = row_pass.reshape(row_count // TILE, BAND, col_count // TILE, TILE)
    return jnp.einsum("xayj,bj->xayb", row_pass, dct_basis, precision=lax.Precision.HIGHEST)


def expand(band_coeffs, dct_basis):
    row_tiles, _, col_tiles, _ = band_coeffs.shape
    col_pass = jnp.einsum("xayb,bj->xayj", band_coeffs, dct_basis, precision=lax.Precision.HIGHEST)
    col_pass = col_pass.reshape(row_tiles, BAND, col_tiles * TILE)
    full = jnp.einsum("ai,xaz->xiz", dct_basis, col_pass, precision=lax.Precision.HIGHEST)
    return full.reshape(row_tiles * TILE, col_tiles * TILE)


def shards(hidden, out_grad, token_mask, momentum):
    chosen = token_mask[:, None] == 1
    weighted = jnp.where(chosen, out_grad, jnp.zeros_like(out_grad))
    grad = lax.dot_general(
        hidden,
        lax.all_gather(weighted, "tensor", axis=1, tiled=True),
        (((0,), (0,)), ((), ())),
        preferred_element_type=jnp.float32,
    )
    accumulated = decay_rate * momentum[0].astype(jnp.float32) + grad
    dct_basis = make_basis()
    band_coeffs = band_of(accumulated, dct_basis)
    momentum_out = (accumulated - expand(band_coeffs, dct_basis)).astype(jnp.bfloat16)[None]
    band_total = lax.psum(band_coeffs, "replica")
    band_update = expand(band_total, dct_basis).astype(jnp.bfloat16)
    return (momentum_out, band_update)


def solution(mesh):
    placed = (
        P("replica", "tensor"),
        P("replica", "tensor"),
        P("replica"),
        P("replica", "tensor", None),
    )
    return jax.shard_map(
        shards,
        mesh=mesh,
        in_specs=placed,
        out_specs=(P("replica", "tensor", None), P("tensor", None)),
        check_vma=False,
    )
```

profile of v0, /device:TPU:24, one launch (start us, length us, event | category | flops | bytes accessed | tf_op | source)
XLA Modules:
  0.0 389.3 jit_solution(8546037379982481973)
XLA Ops:
  7.2 0.0 copy-start
  7.2 0.0 all-gather.2.cloned.1.call-start
  7.2 0.8 broadcast_compare_fusion
  8.1 1.8 broadcast_select_fusion
  9.9 0.0 all-gather.2.cloned.1.call-update
  9.9 51.7 %all-gather.2.cloned.1.call-done = bf16[1024,1792]{0,1:T(8,128)(2,1)} async-done(((bf16[1024,224]{0,1:T(8,128)(2,1)}), bf16[1024,1792]{0,1:T(8,128)(2,1)}) %all-gather.2.cloned.1.call-update) | async-done | bytes 3670032 | tf_op jit(solution)/shard_map/all_gather | solution.py:43
  61.6 0.0 copy-done
  61.6 7.6 %bitcast_add_fusion = f32[1216,1792]{1,0:T(8,128)S(1)} fusion(bf16[1,1216,1792]{2,1,0:T(8,128)(2,1)} %param.7, bf16[1024,1792]{0,1:T(8,128)(2,1)} %all-gather.2.cloned.1.call-done, bf16[1024,1216]{0,1:T(8,128)(2,1)S(1)} %copy-done), kind=kOutput, calls=%fused_computation.2 | convolution fusion | flops 4469276672 | bytes 19234816 | tf_op jit(solution)/shard_map/dot_general | solution.py:41
  69.3 0.0 copy-start.1
  69.3 3.4 copy-done.1
  72.7 5.6 %convolution_bitcast_fusion = f32[19,8,1792]{2,1,0:T(8,128)} fusion(f32[19,64,1792]{2,1,0:T(8,128)S(1)} %bitcast.41, f32[64]{0:T(128)S(1)} %add_multiply_fusion, f32[8]{0:T(128)S(1)} %compare_select_fusion), kind=kOutput, calls=%fused_computation.4 | convolution fusion | flops 209192448 | bytes 9806112 | tf_op jit(solution)/shard_map/ai,xiz->xaz/dot_general | solution.py:25
  78.3 3.1 reshape.41
  81.4 11.4 %fusion.5 = f32[19,8,28,8]{2,3,1,0:T(8,128)S(1)} fusion(f32[19,8,28,64]{3,2,1,0:T(8,128)} %reshape.41, f32[64]{0:T(128)S(1)} %add_multiply_fusion, f32[8]{0:T(128)S(1)} %compare_select_fusion), kind=kOutput, calls=%fused_computation.10 | convolution fusion | flops 26150400 | bytes 1226016 | tf_op jit(solution)/shard_map/xayj,bj->xayb/dot_general | solution.py:27
  92.9 0.0 copy-start.2
  92.9 5.6 %fusion.3 = f32[19,8,28,64]{3,2,1,0:T(8,128)} fusion(f32[19,8,28,8]{2,3,1,0:T(8,128)S(1)} %fusion.5, f32[64]{0:T(128)S(1)} %add_multiply_fusion, f32[8]{0:T(128)S(1)} %compare_select_fusion), kind=kOutput, calls=%fused_computation.8 | convolution fusion | flops 26150400 | bytes 1226016 | tf_op jit(solution)/shard_map/xayb,bj->xayj/dot_general | solution.py:32
  98.4 0.0 all-reduce.2.cloned.1.call-start
  98.4 3.0 reshape.42
  101.4 0.0 copy-done.2
  101.4 0.0 all-reduce.2.cloned.1.call-update
  101.4 10.5 %fusion.8 = f32[19,1792,64]{1,2,0:T(8,128)} fusion(f32[19,8,1792]{2,1,0:T(8,128)} %reshape.42, f32[64]{0:T(128)S(1)} %add_multiply_fusion, f32[8]{0:T(128)S(1)} %compare_select_fusion), kind=kOutput, calls=%fused_computation.13 | convolution fusion | flops 209192448 | bytes 9806112 | tf_op jit(solution)/shard_map/ai,xaz->xiz/dot_general | solution.py:34
  111.9 9.1 %fusion = bf16[1216,1792]{1,0:T(8,128)(2,1)} fusion(f32[1216,1792]{1,0:T(8,128)} %copy-done.1, f32[19,1792,64]{1,2,0:T(8,128)} %fusion.8), kind=kLoop, calls=%fused_computation.1 | loop fusion | flops 4358144 | bytes 21790720 | tf_op jit(solution)/shard_map/convert_element_type | solution.py:50
  121.1 242.1 %all-reduce.2.cloned.1.call-done = f32[19,8,28,8]{2,3,1,0:T(8,128)} async-done(((f32[19,8,28,8]{2,3,1,0:T(8,128)}), f32[19,8,28,8]{2,3,1,0:T(8,128)}) %all-reduce.2.cloned.1.call-update) | async-done | bytes 136208 | tf_op jit(solution)/shard_map/psum | solution.py:51
  363.1 6.6 %fusion.1 = f32[19,8,28,64]{3,2,1,0:T(8,128)} fusion(f32[19,8,28,8]{2,3,1,0:T(8,128)} %all-reduce.2.cloned.1.call-done, f32[64]{0:T(128)S(1)} %add_multiply_fusion, f32[8]{0:T(128)S(1)} %compare_select_fusion), kind=kOutput, calls=%fused_computation.6 | convolution fusion | flops 26150400 | bytes 1226016 | tf_op jit(solution)/shard_map/xayb,bj->xayj/dot_general | solution.py:32
  369.8 3.0 reshape.44
  372.7 9.7 %convolution_convert_fusion = bf16[19,1792,64]{1,2,0:T(8,128)(2,1)} fusion(f32[19,8,1792]{2,1,0:T(8,128)} %reshape.44, f32[64]{0:T(128)S(1)} %add_multiply_fusion, f32[8]{0:T(128)S(1)} %compare_select_fusion), kind=kOutput, calls=%fused_computation.3 | convolution fusion | flops 211371520 | bytes 5447968 | tf_op jit(solution)/shard_map/ai,xaz->xiz/dot_general | solution.py:34
  (2 shorter events, 0.0 us)
Async XLA Ops:
  7.2 54.5 %copy-start = (bf16[1024,1216]{0,1:T(8,128)(2,1)S(1)}, bf16[1024,1216]{0,1:T(8,128)(2,1)}, u32[]{:S(2)}) copy-start(bf16[1024,1216]{0,1:T(8,128)(2,1)} %param.4) | copy-start | bytes 7471108
  7.2 54.5 %all-gather.2.cloned.1.call-start = ((), (), s32[]{:S(2)}) async-start(), calls=%async_computation | async-start | bytes 4128768 | tf_op jit(solution)/shard_map/all_gather | solution.py:43
  69.3 3.4 copy-start.1
  92.9 8.5 %copy-start.2 = (f32[19,8,28,8]{2,3,1,0:T(8,128)}, f32[19,8,28,8]{2,3,1,0:T(8,128)S(1)}, u32[]{:S(2)}) copy-start(f32[19,8,28,8]{2,3,1,0:T(8,128)S(1)} %fusion.5) | copy-start | bytes 408580
  98.4 264.7 %all-reduce.2.cloned.1.call-start = ((), (), s32[]{:S(2)}) async-start(), calls=%async_computation.1 | async-start | bytes 1245184 | tf_op jit(solution)/shard_map/psum | solution.py:51
Sparse Core Ops, SparseCore 0:
  10.4 51.2 all-gather.1
  101.9 261.2 all-reduce.1
where the time goes:
time: 390 us; the launch traced here: 389 us
  waiting for transfers between devices  294 us (75%)
  matrix products  57.1 us (15%)
  between operations  14.1 us (4%)
  local copies, waits for them, and re-layouts  12.4 us (3%)
  other arithmetic  11.8 us (3%)
    psum x1, waiting for transfers between devices, shards(): band_total = lax.psum(band_coeffs, 'replica')  242 us
    all_gather x1, waiting for transfers between devices, shards(): lax.all_gather(weighted, 'tensor', axis=1, tiled=True)  51.7 us
    dot_general x2, matrix products, expand(): jnp.einsum('ai,xaz->xiz', dct_basis, col_pass, precision=lax.Precision.HI...  20.2 us
    dot_general x2, matrix products, expand(): jnp.einsum('xayb,bj->xayj', band_coeffs, dct_basis, precision=lax.Precisi...  12.2 us
    dot_general x1, matrix products, band_of(): jnp.einsum('xayj,bj->xayb', row_pass, dct_basis, precision=lax.Precision....  11.4 us
    convert_element_type x1, other arithmetic, shards(): (accumulated - expand(band_coeffs, dct_basis)).astype(jnp.bfloat16)[None]  9.13 us
  transfers between devices with their start and end apart: 2, of which 2 were waited for; matrix products, arithmetic and copies ran while one was open for 5% of the time, Pallas kernels for 0%

commit v1 on v0

v1 whole, which is shorter than its diff:
```python
import functools

import jax
import jax.numpy as jnp
import ml_dtypes
import numpy as np
from jax import lax
from jax.experimental import pallas as pl
from jax.experimental.pallas import tpu as pltpu
from jax.sharding import PartitionSpec as P

TILE, BAND = 64, 8
DECAY = 0.9
TOK, DW = 1024, 1792
ROWS, COLS = 1216, 224
CHUNK = 256
NB = DW // CHUNK
NA = -(-ROWS // CHUNK)
BROWS = NA * 32
BCOLS = DW // TILE * BAND
LIVE = 640
FLAG_ROW = BROWS - 1
F32, BF16 = jnp.float32, jnp.bfloat16
MIB = 1 << 20


def _basis():
    k = np.arange(BAND)[:, None]
    n = np.arange(TILE)[None]
    scale = np.where(k == 0, np.sqrt(1.0 / TILE), np.sqrt(2.0 / TILE))
    return (scale * np.cos(np.pi * (2 * n + 1) * k / (2 * TILE))).astype(np.float32)


def _split(a):
    hi = a.astype(ml_dtypes.bfloat16)
    lo = (a - hi.astype(np.float32)).astype(ml_dtypes.bfloat16)
    return hi, lo


def _constants():
    d = _basis()
    block = np.kron(np.eye(4, dtype=np.float32), d)
    hi, lo = _split(block)
    rows_down = np.concatenate([hi, lo], 0)
    rows_up = np.concatenate([hi, hi, lo, lo], 0).T.copy()
    full_hi, full_lo = _split(np.kron(np.eye(DW // TILE, dtype=np.float32), d))
    seven = np.kron(np.eye(7, dtype=np.float32), d)
    local = []
    for odd in range(2):
        part = seven[24 * odd : 24 * odd + 32, COLS * odd : COLS * odd + COLS]
        local.append(np.concatenate(_split(part), 0))
    return dict(
        rows_down=rows_down,
        rows_up=rows_up,
        full_hi=full_hi,
        full_lo=full_lo,
        local=np.stack(local),
    )


CONST = _constants()


def _dot(a, b, ca=1, cb=0):
    return lax.dot_general(a, b, (((ca,), (cb,)), ((), ())), preferred_element_type=F32)


def _halves(x):
    hi = x.astype(BF16)
    return hi, (x - hi.astype(F32)).astype(BF16)


def _place_live(mask, live):
    ones = (mask == 1).astype(F32)
    at = lax.broadcasted_iota(jnp.int32, (128, 128), 0)
    to = lax.broadcasted_iota(jnp.int32, (128, 128), 1)
    upto = _dot(ones.astype(BF16), (at <= to).astype(BF16))
    slot = lax.broadcasted_iota(jnp.int32, (live, 128), 0).astype(F32)
    before = jnp.zeros((1, 1), F32)
    parts = []
    for s in range(TOK // 128):
        place = upto[s : s + 1, :] + before - 1.0
        place = jnp.where(ones[s : s + 1, :] > 0.5, place, -1.0)
        parts.append(jnp.where(slot == place, 1.0, 0.0).astype(BF16))
        before = before + upto[s : s + 1, 127:128]
    return jnp.concatenate(parts, 1), before


def _expand_setup(band, full_hi, full_lo, stack):
    b_hi, b_lo = _halves(band)
    wide = _dot(b_hi, full_hi[...]) + _dot(b_lo, full_hi[...]) + _dot(b_hi, full_lo[...])
    hi, lo = _halves(wide)
    for a in range(NA):
        for q, part in enumerate((hi, lo, hi, lo)):
            stack[a, 32 * q : 32 * q + 32, :] = part[32 * a : 32 * a + 32, :]


def _weights_kernel(live, parity, mask, cot, local, out_w, out_p, out_n):
    onehot, count = _place_live(mask[...], live)
    picked = _dot(cot[...], onehot, 0, 1).astype(BF16)
    out_w[...] = picked
    both = _dot(local[parity[0]], picked)
    out_p[...] = both[:32] + both[32:]
    out_n[...] = jnp.broadcast_to(count, (8, 128))


def _hidden_kernel(live, mask, hid, rows_down, out_h, out_p):
    onehot, _ = _place_live(mask[...], live)
    for a in range(NA):
        n = min(CHUNK, ROWS - a * CHUNK)
        picked = _dot(hid[:, a * CHUNK : a * CHUNK + n], onehot, 0, 1).astype(BF16)
        out_h[a * CHUNK : a * CHUNK + n, :] = picked
        both = _dot(rows_down[:, :n], picked)
        out_p[32 * a : 32 * a + 32, :] = both[:32] + both[32:]


def _momentum_band_kernel(mom, full_hi, full_lo, rows_down, out):
    down = rows_down[...]
    for a in range(NA):
        n = min(CHUNK, ROWS - a * CHUNK)
        part = mom[a * CHUNK : a * CHUNK + n, :]
        cols = _dot(part, full_hi[...], 1, 1) + _dot(part, full_lo[...], 1, 1)
        hi, lo = _halves(cols)
        both = _dot(down[:, :n], hi)
        out[32 * a : 32 * a + 32, :] = both[:32] + both[32:] + _dot(down[:32, :n], lo)


def _band_kernel(live, places, hid_p, mom_band, count, *refs):
    shards, out, cot_p = refs[:8], refs[8], refs[9]
    cot_p[...] = jnp.zeros_like(cot_p)
    for s, shard in enumerate(shards):
        at = pl.ds(pl.multiple_of(places[s], 8), 32)
        cot_p[at, :] += shard[...]
    h_hi, h_lo = _halves(hid_p[...])
    w_hi, w_lo = _halves(cot_p[...])
    grad = _dot(h_hi, w_hi, 1, 1) + _dot(h_lo, w_hi, 1, 1) + _dot(h_hi, w_lo, 1, 1)
    band = DECAY * mom_band[...] + grad
    row = lax.broadcasted_iota(jnp.int32, band.shape, 0)
    over = jnp.where(count[0:1, 0:1] > live + 0.5, 1.0, 0.0)
    out[...] = jnp.where(row == FLAG_ROW, over, band)


def _momentum_kernel(live, places, band, full_hi, full_lo, rows_up, mom, hid, *refs):
    shards, out, cot, stack, sems = refs[:8], refs[8], refs[9], refs[10], refs[11]

    @pl.when(pl.program_id(0) == 0)
    def _():
        copies = []
        for s, shard in enumerate(shards):
            at = pl.ds(pl.multiple_of(places[s], 16), COLS)
            copies.append(pltpu.make_async_copy(shard, cot.at[at, :], sems.at[s]))
        for c in copies:
            c.start()
        _expand_setup(band[...], full_hi, full_lo, stack)
        for c in copies:
            c.wait()

    grad = _dot(hid[...], cot[...], 1, 1)
    kept = grad - _dot(rows_up[...], stack[pl.program_id(0)])
    out[...] = (DECAY * mom[...].astype(F32) + kept).astype(BF16)


def _update_kernel(band, full_hi, full_lo, rows_up, out, stack):
    @pl.when(pl.program_id(0) == 0)
    def _():
        _expand_setup(band[...], full_hi, full_lo, stack)

    out[...] = _dot(rows_up[...], stack[pl.program_id(0)]).astype(BF16)


VM = pl.BlockSpec(memory_space=pltpu.VMEM)
SM = pl.BlockSpec(memory_space=pltpu.SMEM)
HB = pl.BlockSpec(memory_space=pl.ANY)


def _cost(flops, size):
    return pl.CostEstimate(flops=int(flops), bytes_accessed=int(size), transcendentals=0)


def _struct(shape, dtype):
    return jax.ShapeDtypeStruct(shape, dtype)


def _weights(live, parity, mask, cot, local):
    return pl.pallas_call(
        functools.partial(_weights_kernel, live),
        out_shape=(_struct((COLS, live), BF16), _struct((32, live), F32), _struct((8, 128), F32)),
        in_specs=[SM, VM, VM, VM],
        out_specs=(VM, VM, VM),
        compiler_params=pltpu.CompilerParams(vmem_limit_bytes=24 * MIB),
        cost_estimate=_cost(2 * TOK * live * 256, 1 * MIB),
        name="weights",
    )(parity, mask, cot, local)


def _hidden(live, mask, hid, rows_down):
    return pl.pallas_call(
        functools.partial(_hidden_kernel, live),
        out_shape=(_struct((ROWS, live), BF16), _struct((BROWS, live), F32)),
        in_specs=[VM, VM, VM],
        out_specs=(VM, VM),
        compiler_params=pltpu.CompilerParams(vmem_limit_bytes=32 * MIB),
        cost_estimate=_cost(2 * TOK * live * ROWS, 5 * MIB),
        name="hidden",
    )(mask, hid, rows_down)


def _momentum_band(mom, full_hi, full_lo, rows_down):
    return pl.pallas_call(
        _momentum_band_kernel,
        out_shape=_struct((BROWS, BCOLS), F32),
        in_specs=[VM, VM, VM, VM],
        out_specs=VM,
        compiler_params=pltpu.CompilerParams(vmem_limit_bytes=32 * MIB),
        cost_estimate=_cost(4 * ROWS * DW * 256, 6 * MIB),
        name="momentum_band",
    )(mom, full_hi, full_lo, rows_down)


def _band(live, places, hid_p, mom_band, count, shards):
    return pl.pallas_call(
        functools.partial(_band_kernel, live),
        out_shape=_struct((BROWS, BCOLS), F32),
        in_specs=[SM, VM, VM, VM] + [VM] * 8,
        out_specs=VM,
        scratch_shapes=[pltpu.VMEM((BCOLS, live), F32)],
        compiler_params=pltpu.CompilerParams(vmem_limit_bytes=24 * MIB),
        cost_estimate=_cost(6 * BROWS * 256 * live, 2 * MIB),
        name="band",
    )(places, hid_p, mom_band, count, *shards)


def _momentum(live, places, band, full_hi, full_lo, rows_up, mom, hid, shards):
    return pl.pallas_call(
        functools.partial(_momentum_kernel, live),
        out_shape=_struct((ROWS, DW), BF16),
        grid=(NA,),
        in_specs=[SM, VM, VM, VM, VM, pl.BlockSpec((CHUNK, DW), lambda a: (a, 0)), pl.BlockSpec((CHUNK, live), lambda a: (a, 0))]
        + [HB] * 8,
        out_specs=pl.BlockSpec((CHUNK, DW), lambda a: (a, 0)),
        scratch_shapes=[
            pltpu.VMEM((DW, live), BF16),
            pltpu.VMEM((NA, 128, DW), BF16),
            pltpu.SemaphoreType.DMA((8,)),
        ],
        compiler_params=pltpu.CompilerParams(vmem_limit_bytes=40 * MIB, dimension_semantics=("arbitrary",)),
        cost_estimate=_cost(2 * ROWS * DW * (live + 128), 14 * MIB),
        name="momentum",
    )(places, band, full_hi, full_lo, rows_up, mom, hid, *shards)


def _update(band, full_hi, full_lo, rows_up):
    return pl.pallas_call(
        _update_kernel,
        out_shape=_struct((ROWS, DW), BF16),
        grid=(NA,),
        in_specs=[VM, VM, VM, VM],
        out_specs=pl.BlockSpec((CHUNK, DW), lambda a: (a, 0)),
        scratch_shapes=[pltpu.VMEM((NA, 128, DW), BF16)],
        compiler_params=pltpu.CompilerParams(vmem_limit_bytes=24 * MIB, dimension_semantics=("arbitrary",)),
        cost_estimate=_cost(2 * ROWS * DW * 256, 6 * MIB),
        name="update",
    )(band, full_hi, full_lo, rows_up)


def _tensor_shift(a, dx, dy):
    pairs = [(x * 4 + y, (x + dx) % 2 * 4 + (y + dy) % 4) for x in range(2) for y in range(4)]
    return lax.ppermute(a, "tensor", pairs)


def _replica_shift(a, df, dz, dc):
    pairs = [
        (f * 16 + z * 2 + c, (f + df) % 2 * 16 + (z + dz) % 8 * 2 + (c + dc) % 2)
        for f in range(2)
        for z in range(8)
        for c in range(2)
    ]
    return lax.ppermute(a, "replica", pairs)


SHIFTS = ((0, 0), (0, 1), (0, 3), (1, 0), (0, 2), (1, 1), (1, 3), (1, 2))


def _gather_direct(a):
    return [a if s == (0, 0) else _tensor_shift(a, *s) for s in SHIFTS]


def _gather(a):
    up, down = _tensor_shift(a, 0, 1), _tensor_shift(a, 0, 3)
    across = _tensor_shift(a, 1, 0)
    two = _tensor_shift(a, 0, 2)
    return [a, up, down, across, two, _tensor_shift(up, 1, 0), _tensor_shift(down, 1, 0), _tensor_shift(across, 0, 2)]


def _sum_replicas(band):
    core = lax.axis_index("replica") % 2
    half = BROWS // 2
    mine = lax.dynamic_slice(band, (core * half, 0), (half, BCOLS))
    other = lax.dynamic_slice(band, ((1 - core) * half, 0), (half, BCOLS))
    one = mine + _replica_shift(other, 0, 0, 1)
    below, above = _replica_shift(one, 0, 1, 0), _replica_shift(one, 0, 7, 0)
    two, three = one + above, one + below + above
    eight = three + _replica_shift(three, 0, 5, 0) + _replica_shift(two, 0, 3, 0)
    whole = eight + _replica_shift(eight, 1, 0, 0)
    back = _replica_shift(whole, 0, 0, 1)
    first, second = jnp.where(core == 0, whole, back), jnp.where(core == 0, back, whole)
    return jnp.concatenate([first, second], 0)


def _step(live, hidden, out_grad, mask, mom):
    c = {k: jnp.asarray(v) for k, v in CONST.items()}
    index = lax.axis_index("tensor")
    x, y = index // 4, index % 4
    owners = [(x + dx) % 2 * 4 + (y - dy) % 4 for dx, dy in SHIFTS]
    places = jnp.stack([o * COLS for o in owners]).astype(jnp.int32)
    band_places = jnp.stack([o // 2 * 56 + o % 2 * 24 for o in owners]).astype(jnp.int32)
    parity = (index % 2).astype(jnp.int32).reshape(1)

    cot, cot_p, count = _weights(live, parity, mask, out_grad, c["local"])
    cot_ps = _gather_direct(cot_p)
    hid, hid_p = _hidden(live, mask, hidden, c["rows_down"])
    mom_band = _momentum_band(mom, c["full_hi"], c["full_lo"], c["rows_down"])
    band = _band(live, band_places, hid_p, mom_band, count, cot_ps)
    cots = _gather(cot)
    total = _sum_replicas(band)
    momentum_out = _momentum(live, places, band, c["full_hi"], c["full_lo"], c["rows_up"], mom, hid, cots)
    band_update = _update(total, c["full_hi"], c["full_lo"], c["rows_up"])
    return momentum_out, band_update, total[FLAG_ROW, 0]


def shards(hidden, out_grad, token_mask, momentum):
    mask = token_mask.reshape(8, 128)
    mom = momentum[0]
    state = _step(LIVE, hidden, out_grad, mask, mom)
    momentum_out, band_update, _ = lax.while_loop(
        lambda s: s[2] > 0.5,
        lambda s: _step(TOK, hidden, out_grad, mask, mom),
        state,
    )
    return momentum_out[None], band_update


def solution(mesh):
    placed = (P("replica", "tensor"), P("replica", "tensor"), P("replica"), P("replica", "tensor", None))
    return jax.shard_map(
        shards,
        mesh=mesh,
        in_specs=placed,
        out_specs=(P("replica", "tensor", None), P("tensor", None)),
        check_vma=False,
    )
```

time: 390 us -> 106 us (0.27)
  waiting for transfers between devices: 294 us -> 17.4 us
  matrix products: 57.1 us -> 0 us
  starting transfers between devices: 0.04 us -> 35.9 us
  Pallas kernels: 0 us -> 31.1 us
  between operations: 14.1 us -> 1.09 us
  other arithmetic: 11.8 us -> 0.97 us
  local copies, waits for them, and re-layouts: 12.4 us -> 17.3 us
    psum x1 -> x0, waiting for transfers between devices: 242 us -> none  [shards(): band_total = lax.psum(band_coeffs, 'replica')]
    dot_general x7 -> x0, matrix products: 57.1 us -> none  [the longest x2 20.2 us: expand(): jnp.einsum('ai,xaz->xiz', dct_basis, col_pass, precision=lax.Precision.HI...]
    all_gather x1 -> x0, waiting for transfers between devices: 51.7 us -> none  [shards(): lax.all_gather(weighted, 'tensor', axis=1, tiled=True)]
    ppermute x0 -> x21, starting transfers between devices: none -> 35.9 us  [the longest x14 21.6 us: _tensor_shift(): return lax.ppermute(a, 'tensor', pairs)]
    pallas_call x0 -> x6, Pallas kernels: none -> 31.1 us  [the longest x1 9.91 us: _momentum(): pl.pallas_call(functools.partial(_momentum_kernel, live), out_shape=_stru...]
    ppermute x0 -> x21, waiting for transfers between devices: none -> 17.4 us  [the longest x7 10.4 us: _replica_shift(): return lax.ppermute(a, 'replica', pairs)]
    unnamed x6 -> x48, local copies, waits for them, and re-layouts: 3.38 us -> 16 us
    convert_element_type x1 -> x0, other arithmetic: 9.13 us -> none  [shards(): (accumulated - expand(band_coeffs, dct_basis)).astype(jnp.bfloat16)[None]]
  transfers between devices with their start and end apart: 2 -> 21, of which waited for: 2 -> 6; matrix products, arithmetic and copies ran while one was open for 5% -> 6% of each run, Pallas kernels for 0% -> 17%
where the time goes in v1:
time: 106 us; the launch traced here: 105 us
  starting transfers between devices  35.9 us (34%)
  Pallas kernels  31.1 us (29%)
  waiting for transfers between devices  17.4 us (16%)
  local copies, waits for them, and re-layouts  17.3 us (16%)
  between operations  1.09 us (1%)
    ppermute x14, starting transfers between devices, _tensor_shift(): return lax.ppermute(a, 'tensor', pairs)  21.6 us
    unnamed x48, local copies, waits for them, and re-layouts  16 us
    ppermute x7, starting transfers between devices, _replica_shift(): return lax.ppermute(a, 'replica', pairs)  14.3 us
    ppermute x7, waiting for transfers between devices, _replica_shift(): return lax.ppermute(a, 'replica', pairs)  10.4 us
    pallas_call x1, Pallas kernels, _momentum(): pl.pallas_call(functools.partial(_momentum_kernel, live), out_shape=_stru...  9.91 us
    pallas_call x1, Pallas kernels, _momentum_band(): pl.pallas_call(_momentum_band_kernel, out_shape=_struct((BROWS, BCOLS), F...  7.89 us
    ppermute x14, waiting for transfers between devices, _tensor_shift(): return lax.ppermute(a, 'tensor', pairs)  6.95 us
    pallas_call x1, Pallas kernels, _hidden(): pl.pallas_call(functools.partial(_hidden_kernel, live), out_shape=(_struc...  5.63 us
  transfers between devices with their start and end apart: 21, of which 6 were waited for; matrix products, arithmetic and copies ran while one was open for 6% of the time, Pallas kernels for 17%

profile of v1, /device:TPU:24, one launch (start us, length us, event | category | flops | bytes accessed | tf_op | source)
XLA Modules:
  0.0 104.7 jit_solution(2701184773280447182)
XLA Ops:
  0.6 1.2 %copy.12.cot = bf16[1024,224]{1,0:T(8,128)(2,1)S(1)} copy(bf16[1024,224]{0,1:T(8,128)(2,1)} %param.12) | data formatting | bytes 917504 | tf_op args[1]
  1.9 0.9 copy-done.16
  2.8 1.7 %weights.6 = (bf16[224,640]{1,0:T(8,128)(2,1)S(1)}, f32[32,640]{1,0:T(8,128)S(1)}, f32[8,128]{1,0:T(8,128)S(1)}) custom-call(s32[1]{0:T(128)} %bitcast.18.parity, s32[8,128]{1,0:T(8,128)} %bitcast.79, bf16[1024,224]{1,0:T(8,128)(2,1)S(1)} %copy.12.cot, bf16[2,64,224]{2,1,0:T(8,128)(2,1)S(1)} %copy-done.16), custom_call_target="tpu_custom_call" | custom-call | flops 335544320 | bytes 1048576 | tf_op jit(solution)/shard_map/weights/pallas_call | solution.py:185
  4.5 0.7 copy-done.4
  5.2 0.6 copy-done.13
  5.8 2.2 %collective-permute-start.27 = (f32[32,640]{1,0:T(8,128)S(1)}, f32[32,640]{1,0:T(8,128)S(1)}, u32[]{:S(2)}, u32[]{:S(2)}) collective-permute-start(f32[32,640]{1,0:T(8,128)S(1)} %get-tuple-element.209.refs_0_), channel_id=1, source_target_pairs={{0,6},{1,7},{2,4},{3,5},{4,2},{5,3},{6,0},{7,1},{8,14},{9,15},{10,... | collective-permute-start | bytes 245768 | tf_op jit(solution)/shard_map/ppermute | solution.py:268
  8.0 1.6 %collective-permute-start.26 = (f32[32,640]{1,0:T(8,128)S(1)}, f32[32,640]{1,0:T(8,128)S(1)}, u32[]{:S(2)}, u32[]{:S(2)}) collective-permute-start(f32[32,640]{1,0:T(8,128)S(1)} %get-tuple-element.209.refs_0_), channel_id=1, source_target_pairs={{0,7},{1,4},{2,5},{3,6},{4,3},{5,0},{6,1},{7,2},{8,15},{9,12},{10,... | collective-permute-start | bytes 245768 | tf_op jit(solution)/shard_map/ppermute | solution.py:268
  9.5 2.6 %collective-permute-start.25 = (f32[32,640]{1,0:T(8,128)S(1)}, f32[32,640]{1,0:T(8,128)S(1)}, u32[]{:S(2)}, u32[]{:S(2)}) collective-permute-start(f32[32,640]{1,0:T(8,128)S(1)} %get-tuple-element.209.refs_0_), channel_id=1, source_target_pairs={{0,5},{1,6},{2,7},{3,4},{4,1},{5,2},{6,3},{7,0},{8,13},{9,14},{10,... | collective-permute-start | bytes 245768 | tf_op jit(solution)/shard_map/ppermute | solution.py:268
  12.1 1.1 %collective-permute-start.24 = (f32[32,640]{1,0:T(8,128)S(1)}, f32[32,640]{1,0:T(8,128)S(1)}, u32[]{:S(2)}, u32[]{:S(2)}) collective-permute-start(f32[32,640]{1,0:T(8,128)S(1)} %get-tuple-element.209.refs_0_), channel_id=1, source_target_pairs={{0,2},{1,3},{2,0},{3,1},{4,6},{5,7},{6,4},{7,5},{8,10},{9,11},{10,... | collective-permute-start | bytes 245768 | tf_op jit(solution)/shard_map/ppermute | solution.py:268
  13.2 1.1 %copy-done = bf16[224,1792]{1,0:T(8,128)(2,1)S(1)} copy-done((bf16[224,1792]{1,0:T(8,128)(2,1)S(1)}, bf16[224,1792]{1,0:T(8,128)(2,1)}, u32[]{:S(2)}) %copy-start) | copy-done | bytes 802840
  14.3 1.1 %copy-done.2 = bf16[224,1792]{1,0:T(8,128)(2,1)S(1)} copy-done((bf16[224,1792]{1,0:T(8,128)(2,1)S(1)}, bf16[224,1792]{1,0:T(8,128)(2,1)}, u32[]{:S(2)}) %copy-start.2) | copy-done | bytes 802840
  15.5 0.8 copy-done.17
  16.2 7.9 %momentum_band.2.mom_band = f32[160,224]{1,0:T(8,128)} custom-call(bf16[1216,1792]{1,0:T(8,128)(2,1)} %bitcast.75, bf16[224,1792]{1,0:T(8,128)(2,1)S(1)} %copy-done.2, bf16[224,1792]{1,0:T(8,128)(2,1)S(1)} %copy-done, bf16[64,256]{1,0:T(8,128)(2,1)S(1)} %copy-done.17), custom_call_target="tpu_custom_call" | custom-call | flops 2231369728 | bytes 6291456 | tf_op jit(solution)/shard_map/momentum_band/pallas_call | solution.py:209
  24.1 4.4 %copy.11.hid = bf16[1024,1216]{1,0:T(8,128)(2,1)} copy(bf16[1024,1216]{0,1:T(8,128)(2,1)} %param.11) | data formatting | bytes 4980736 | tf_op args[0]
  28.5 0.6 stack.189.places
  29.1 0.6 collective-permute-start.23
  29.8 0.7 collective-permute-start.22
  30.5 0.6 copy-done.7
  31.1 2.5 %collective-permute-start.21 = (f32[32,640]{1,0:T(8,128)S(1)}, f32[32,640]{1,0:T(8,128)S(1)}, u32[]{:S(2)}, u32[]{:S(2)}) collective-permute-start(f32[32,640]{1,0:T(8,128)S(1)} %get-tuple-element.209.refs_0_), channel_id=1, source_target_pairs={{0,1},{1,2},{2,3},{3,0},{4,5},{5,6},{6,7},{7,4},{8,9},{9,10},{10,1... | collective-permute-start | bytes 245768 | tf_op jit(solution)/shard_map/ppermute | solution.py:268
  33.6 0.8 copy-done.18
  34.4 5.6 %hidden.6 = (bf16[1216,640]{1,0:T(8,128)(2,1)S(1)}, f32[160,640]{1,0:T(8,128)S(1)}) custom-call(s32[8,128]{1,0:T(8,128)} %bitcast.80, bf16[1024,1216]{1,0:T(8,128)(2,1)} %copy.11.hid, bf16[64,256]{1,0:T(8,128)(2,1)S(1)} %copy-done.18), custom_call_target="tpu_custom_call" | custom-call | flops 1593835520 | bytes 5242880 | tf_op jit(solution)/shard_map/hidden/pallas_call | solution.py:197
  40.0 0.6 copy-done.9
  40.7 0.6 copy-done.11
  41.3 0.9 copy-done.10
  42.2 0.9 copy-done.12
  43.1 0.7 copy-done.14
  43.8 1.6 %band.6 = f32[160,224]{1,0:T(8,128)S(1)} custom-call(s32[8]{0:T(128)S(1)} %copy-done.15, f32[160,640]{1,0:T(8,128)S(1)} %get-tuple-element.207.hid_p, f32[160,224]{1,0:T(8,128)} %momentum_band.2.mom_band, f32[8,128]{1,0:T(8,128)S(1)} %copy-done.14, f32[32,640]{1,0:T(8,128)S(1)} %get-tuple-element.209.refs_0_, f32[32,640]{1,0:T(8,128)S(1)} %collective-permute-done.21.refs_1_, ...), custom_call_target="tpu_custom_call" | custom-call | flops 157286400 | bytes 2097152 | tf_op jit(solution)/shard_map/band/pallas_call | solution.py:221
  45.4 0.4 collective-permute-start.35
  45.8 1.3 %collective-permute-done.35 = f32[80,224]{1,0:T(8,128)S(1)} collective-permute-done((f32[80,224]{1,0:T(8,128)S(1)}, f32[80,224]{1,0:T(8,128)S(1)}, u32[]{:S(2)}, u32[]{:S(2)}) %collective-permute-start.35) | collective-permute-done | bytes 71712 | tf_op jit(solution)/shard_map/ppermute | solution.py:278
  47.0 5.9 %collective-permute-start.37 = (f32[80,224]{1,0:T(8,128)S(1)}, f32[80,224]{1,0:T(8,128)S(1)}, u32[]{:S(2)}, u32[]{:S(2)}) collective-permute-start(f32[80,224]{1,0:T(8,128)S(1)} %dynamic-slice_add_fusion.1), channel_id=1, source_target_pairs={{0,112},{8,120},{16,0},{24,8},{32,16},{40,24},{48,32},{56,40},{64,... | collective-permute-start | bytes 215048 | tf_op jit(solution)/shard_map/ppermute | solution.py:278
  53.0 2.1 %collective-permute-done.37 = f32[80,224]{1,0:T(8,128)S(1)} collective-permute-done((f32[80,224]{1,0:T(8,128)S(1)}, f32[80,224]{1,0:T(8,128)S(1)}, u32[]{:S(2)}, u32[]{:S(2)}) %collective-permute-start.37) | collective-permute-done | bytes 71712 | tf_op jit(solution)/shard_map/ppermute | solution.py:278
  55.0 3.6 %collective-permute-done.36 = f32[80,224]{1,0:T(8,128)S(1)} collective-permute-done((f32[80,224]{1,0:T(8,128)S(1)}, f32[80,224]{1,0:T(8,128)S(1)}, u32[]{:S(2)}, u32[]{:S(2)}) %collective-permute-start.36) | collective-permute-done | bytes 71712 | tf_op jit(solution)/shard_map/ppermute | solution.py:278
  58.7 5.0 %collective-permute-start.38 = (f32[80,224]{1,0:T(8,128)S(1)}, f32[80,224]{1,0:T(8,128)S(1)}, u32[]{:S(2)}, u32[]{:S(2)}) collective-permute-start(f32[80,224]{1,0:T(8,128)S(1)} %get-tuple-element.283), channel_id=1, source_target_pairs={{0,80},{8,88},{16,96},{24,104},{32,112},{40,120},{48,0},{56,8},{64... | collective-permute-start | bytes 215048 | tf_op jit(solution)/shard_map/ppermute | solution.py:278
  63.7 1.5 %collective-permute-start.30 = (bf16[224,640]{1,0:T(8,128)(2,1)}, bf16[224,640]{1,0:T(8,128)(2,1)}, u32[]{:S(2)}, u32[]{:S(2)}) collective-permute-start(bf16[224,640]{1,0:T(8,128)(2,1)} %copy-done.4), channel_id=1, source_target_pairs={{0,4},{1,5},{2,6},{3,7},{4,0},{5,1},{6,2},{7,3},{8,12},{9,13},{10,... | collective-permute-start | bytes 860168 | tf_op jit(solution)/shard_map/ppermute | solution.py:268
  65.2 3.2 %collective-permute-start.28 = (bf16[224,640]{1,0:T(8,128)(2,1)}, bf16[224,640]{1,0:T(8,128)(2,1)}, u32[]{:S(2)}, u32[]{:S(2)}) collective-permute-start(bf16[224,640]{1,0:T(8,128)(2,1)} %copy-done.4), channel_id=1, source_target_pairs={{0,1},{1,2},{2,3},{3,0},{4,5},{5,6},{6,7},{7,4},{8,9},{9,10},{10,1... | collective-permute-start | bytes 860168 | tf_op jit(solution)/shard_map/ppermute | solution.py:268
  68.5 2.8 %collective-permute-start.40 = (f32[80,224]{1,0:T(8,128)S(1)}, f32[80,224]{1,0:T(8,128)S(1)}, u32[]{:S(2)}, u32[]{:S(2)}) collective-permute-start(f32[80,224]{1,0:T(8,128)S(1)} %add_add_fusion.2), channel_id=1, source_target_pairs={{0,128},{8,136},{16,144},{24,152},{32,160},{40,168},{48,176},{56,1... | collective-permute-start | bytes 215048 | tf_op jit(solution)/shard_map/ppermute | solution.py:278
  71.3 3.5 %collective-permute-done.40 = f32[80,224]{1,0:T(8,128)S(1)} collective-permute-done((f32[80,224]{1,0:T(8,128)S(1)}, f32[80,224]{1,0:T(8,128)S(1)}, u32[]{:S(2)}, u32[]{:S(2)}) %collective-permute-start.40) | collective-permute-done | bytes 71712 | tf_op jit(solution)/shard_map/ppermute | solution.py:278
  75.0 1.3 %collective-permute-start.31 = (bf16[224,640]{1,0:T(8,128)(2,1)}, bf16[224,640]{1,0:T(8,128)(2,1)S(1)}, u32[]{:S(2)}, u32[]{:S(2)}) collective-permute-start(bf16[224,640]{1,0:T(8,128)(2,1)} %copy-done.4), channel_id=1, source_target_pairs={{0,2},{1,3},{2,0},{3,1},{4,6},{5,7},{6,4},{7,5},{8,10},{9,11},{10,... | collective-permute-start | bytes 860168 | tf_op jit(solution)/shard_map/ppermute | solution.py:268
  76.3 2.3 %collective-permute-start.34 = (bf16[224,640]{1,0:T(8,128)(2,1)}, bf16[224,640]{1,0:T(8,128)(2,1)S(1)}, u32[]{:S(2)}, u32[]{:S(2)}) collective-permute-start(bf16[224,640]{1,0:T(8,128)(2,1)} %collective-permute-done.30.refs_3_), channel_id=1, source_target_pairs={{0,2},{1,3},{2,0},{3,1},{4,6},{5,7},{6,4},{7,5},{8,10},{9,11},{10,... | collective-permute-start | bytes 860168 | tf_op jit(solution)/shard_map/ppermute | solution.py:268
  78.7 0.3 collective-permute-start.33
  78.9 1.8 %collective-permute-start.32 = (bf16[224,640]{1,0:T(8,128)(2,1)}, bf16[224,640]{1,0:T(8,128)(2,1)S(1)}, u32[]{:S(2)}, u32[]{:S(2)}) collective-permute-start(bf16[224,640]{1,0:T(8,128)(2,1)} %collective-permute-done.28.refs_1_), channel_id=1, source_target_pairs={{0,4},{1,5},{2,6},{3,7},{4,0},{5,1},{6,2},{7,3},{8,12},{9,13},{10,... | collective-permute-start | bytes 860168 | tf_op jit(solution)/shard_map/ppermute | solution.py:268
  80.7 0.9 broadcast_select_fusion.3
  81.6 0.6 slice.14
  82.2 4.5 %update.6 = bf16[1216,1792]{1,0:T(8,128)(2,1)} custom-call(f32[160,224]{1,0:T(8,128)S(1)} %pad_maximum_fusion.1.band, bf16[224,1792]{1,0:T(8,128)(2,1)S(1)} %copy-done.3, bf16[224,1792]{1,0:T(8,128)(2,1)S(1)} %copy-done.1, bf16[256,128]{1,0:T(8,128)(2,1)S(1)} %copy-done.6), custom_call_target="tpu_custom_call" | custom-call | flops 1115684864 | bytes 6291456 | tf_op jit(solution)/shard_map/update/pallas_call | solution.py:253
  86.7 5.5 %collective-permute-done.34.refs_7_ = bf16[224,640]{1,0:T(8,128)(2,1)S(1)} collective-permute-done((bf16[224,640]{1,0:T(8,128)(2,1)}, bf16[224,640]{1,0:T(8,128)(2,1)S(1)}, u32[]{:S(2)}, u32[]{:S(2)}) %collective-permute-start.34) | collective-permute-done | bytes 286752 | tf_op jit(solution)/shard_map/ppermute | solution.py:268
  92.2 1.5 %collective-permute-done.32.refs_5_ = bf16[224,640]{1,0:T(8,128)(2,1)S(1)} collective-permute-done((bf16[224,640]{1,0:T(8,128)(2,1)}, bf16[224,640]{1,0:T(8,128)(2,1)S(1)}, u32[]{:S(2)}, u32[]{:S(2)}) %collective-permute-start.32) | collective-permute-done | bytes 286752 | tf_op jit(solution)/shard_map/ppermute | solution.py:268
  93.7 9.9 %momentum.6 = bf16[1216,1792]{1,0:T(8,128)(2,1)} custom-call(s32[8]{0:T(128)S(1)} %stack.180.places, f32[160,224]{1,0:T(8,128)S(1)} %band.6, bf16[224,1792]{1,0:T(8,128)(2,1)S(1)} %copy-done.3, bf16[224,1792]{1,0:T(8,128)(2,1)S(1)} %copy-done.1, bf16[256,128]{1,0:T(8,128)(2,1)S(1)} %copy-done.6, bf16[1216,1792]{1,0:T(8,128)(2,1)} %bitcast.76, ...), custom_call_target="tpu_custom_call" | custom-call | flops 3347054592 | bytes 14680064 | tf_op jit(solution)/shard_map/momentum/pallas_call | solution.py:234
  103.6 0.9 while.16
  (59 shorter events, 0.5 us)
Async XLA Ops:
  1.9 22.3 %copy-start.25 = (bf16[1024,224]{1,0:T(8,128)(2,1)}, bf16[1024,224]{1,0:T(8,128)(2,1)S(1)}, u32[]{:S(2)}) copy-start(bf16[1024,224]{1,0:T(8,128)(2,1)S(1)} %copy.12.cot) | copy-start | bytes 1376260
  1.9 0.9 copy-start.16
  4.5 0.7 copy-start.4
  5.2 0.6 copy-start.13
  5.8 23.9 %collective-permute-start.27 = (f32[32,640]{1,0:T(8,128)S(1)}, f32[32,640]{1,0:T(8,128)S(1)}, u32[]{:S(2)}, u32[]{:S(2)}) collective-permute-start(f32[32,640]{1,0:T(8,128)S(1)} %get-tuple-element.209.refs_0_), channel_id=1, source_target_pairs={{0,6},{1,7},{2,4},{3,5},{4,2},{5,3},{6,0},{7,1},{8,14},{9,15},{10,... | collective-permute-start | bytes 245768 | tf_op jit(solution)/shard_map/ppermute | solution.py:268
  8.0 22.5 %collective-permute-start.26 = (f32[32,640]{1,0:T(8,128)S(1)}, f32[32,640]{1,0:T(8,128)S(1)}, u32[]{:S(2)}, u32[]{:S(2)}) collective-permute-start(f32[32,640]{1,0:T(8,128)S(1)} %get-tuple-element.209.refs_0_), channel_id=1, source_target_pairs={{0,7},{1,4},{2,5},{3,6},{4,3},{5,0},{6,1},{7,2},{8,15},{9,12},{10,... | collective-permute-start | bytes 245768 | tf_op jit(solution)/shard_map/ppermute | solution.py:268
  9.5 30.5 %collective-permute-start.25 = (f32[32,640]{1,0:T(8,128)S(1)}, f32[32,640]{1,0:T(8,128)S(1)}, u32[]{:S(2)}, u32[]{:S(2)}) collective-permute-start(f32[32,640]{1,0:T(8,128)S(1)} %get-tuple-element.209.refs_0_), channel_id=1, source_target_pairs={{0,5},{1,6},{2,7},{3,4},{4,1},{5,2},{6,3},{7,0},{8,13},{9,14},{10,... | collective-permute-start | bytes 245768 | tf_op jit(solution)/shard_map/ppermute | solution.py:268
  12.1 28.6 %collective-permute-start.24 = (f32[32,640]{1,0:T(8,128)S(1)}, f32[32,640]{1,0:T(8,128)S(1)}, u32[]{:S(2)}, u32[]{:S(2)}) collective-permute-start(f32[32,640]{1,0:T(8,128)S(1)} %get-tuple-element.209.refs_0_), channel_id=1, source_target_pairs={{0,2},{1,3},{2,0},{3,1},{4,6},{5,7},{6,4},{7,5},{8,10},{9,11},{10,... | collective-permute-start | bytes 245768 | tf_op jit(solution)/shard_map/ppermute | solution.py:268
  13.2 1.1 %copy-start = (bf16[224,1792]{1,0:T(8,128)(2,1)S(1)}, bf16[224,1792]{1,0:T(8,128)(2,1)}, u32[]{:S(2)}) copy-start(bf16[224,1792]{1,0:T(8,128)(2,1)} %constant.542.clone.full_lo) | copy-start | bytes 2408452
  14.3 1.1 %copy-start.2 = (bf16[224,1792]{1,0:T(8,128)(2,1)S(1)}, bf16[224,1792]{1,0:T(8,128)(2,1)}, u32[]{:S(2)}) copy-start(bf16[224,1792]{1,0:T(8,128)(2,1)} %constant.541.clone.full_hi) | copy-start | bytes 2408452
  15.5 0.8 copy-start.17
  29.1 12.2 %copy-start.15 = (s32[8]{0:T(128)S(1)}, s32[8]{0:T(128)}, u32[]{:S(2)}) copy-start(s32[8]{0:T(128)} %stack.189.places) | copy-start | bytes 100
  29.1 53.1 %copy-start.1 = (bf16[224,1792]{1,0:T(8,128)(2,1)S(1)}, bf16[224,1792]{1,0:T(8,128)(2,1)}, u32[]{:S(2)}) copy-start(bf16[224,1792]{1,0:T(8,128)(2,1)} %constant.542.clone.full_lo) | copy-start | bytes 2408452
  29.1 53.1 %copy-start.3 = (bf16[224,1792]{1,0:T(8,128)(2,1)S(1)}, bf16[224,1792]{1,0:T(8,128)(2,1)}, u32[]{:S(2)}) copy-start(bf16[224,1792]{1,0:T(8,128)(2,1)} %constant.541.clone.full_hi) | copy-start | bytes 2408452
  29.1 53.1 %copy-start.6 = (bf16[256,128]{1,0:T(8,128)(2,1)S(1)}, bf16[256,128]{1,0:T(8,128)(2,1)}, u32[]{:S(2)}) copy-start(bf16[256,128]{1,0:T(8,128)(2,1)} %constant.540.clone.rows_up) | copy-start | bytes 196612
  29.1 12.2 %collective-permute-start.23 = (f32[32,640]{1,0:T(8,128)S(1)}, f32[32,640]{1,0:T(8,128)S(1)}, u32[]{:S(2)}, u32[]{:S(2)}) collective-permute-start(f32[32,640]{1,0:T(8,128)S(1)} %get-tuple-element.209.refs_0_), channel_id=1, source_target_pairs={{0,4},{1,5},{2,6},{3,7},{4,0},{5,1},{6,2},{7,3},{8,12},{9,13},{10,... | collective-permute-start | bytes 245768 | tf_op jit(solution)/shard_map/ppermute | solution.py:268
  29.8 11.6 %collective-permute-start.22 = (f32[32,640]{1,0:T(8,128)S(1)}, f32[32,640]{1,0:T(8,128)S(1)}, u32[]{:S(2)}, u32[]{:S(2)}) collective-permute-start(f32[32,640]{1,0:T(8,128)S(1)} %get-tuple-element.209.refs_0_), channel_id=1, source_target_pairs={{0,3},{1,0},{2,1},{3,2},{4,7},{5,4},{6,5},{7,6},{8,11},{9,8},{10,9... | collective-permute-start | bytes 245768 | tf_op jit(solution)/shard_map/ppermute | solution.py:268
  30.5 0.6 copy-start.7
  31.1 10.2 %collective-permute-start.21 = (f32[32,640]{1,0:T(8,128)S(1)}, f32[32,640]{1,0:T(8,128)S(1)}, u32[]{:S(2)}, u32[]{:S(2)}) collective-permute-start(f32[32,640]{1,0:T(8,128)S(1)} %get-tuple-element.209.refs_0_), channel_id=1, source_target_pairs={{0,1},{1,2},{2,3},{3,0},{4,5},{5,6},{6,7},{7,4},{8,9},{9,10},{10,1... | collective-permute-start | bytes 245768 | tf_op jit(solution)/shard_map/ppermute | solution.py:268
  33.6 0.8 copy-start.18
  34.4 6.9 %copy-start.8 = (f32[32,640]{1,0:T(8,128)S(1)}, f32[32,640]{1,0:T(8,128)}, u32[]{:S(2)}) copy-start(f32[32,640]{1,0:T(8,128)} %copy-done.7) | copy-start | bytes 245764
  40.0 0.6 copy-start.9
  40.7 0.6 copy-start.11
  41.3 0.9 copy-start.10
  42.2 0.9 copy-start.12
  43.1 0.7 copy-start.14
  45.4 1.7 %collective-permute-start.35 = (f32[80,224]{1,0:T(8,128)S(1)}, f32[80,224]{1,0:T(8,128)S(1)}, u32[]{:S(2)}, u32[]{:S(2)}) collective-permute-start(f32[80,224]{1,0:T(8,128)S(1)} %constant_dynamic-slice_fusion.1), channel_id=1, source_target_pairs={{0,8},{8,0},{16,24},{24,16},{32,40},{40,32},{48,56},{56,48},{64,72... | collective-permute-start | bytes 215048 | tf_op jit(solution)/shard_map/ppermute | solution.py:278
  47.0 8.0 %collective-permute-start.37 = (f32[80,224]{1,0:T(8,128)S(1)}, f32[80,224]{1,0:T(8,128)S(1)}, u32[]{:S(2)}, u32[]{:S(2)}) collective-permute-start(f32[80,224]{1,0:T(8,128)S(1)} %dynamic-slice_add_fusion.1), channel_id=1, source_target_pairs={{0,112},{8,120},{16,0},{24,8},{32,16},{40,24},{48,32},{56,40},{64,... | collective-permute-start | bytes 215048 | tf_op jit(solution)/shard_map/ppermute | solution.py:278
  53.0 5.7 %collective-permute-start.36 = (f32[80,224]{1,0:T(8,128)S(1)}, f32[80,224]{1,0:T(8,128)S(1)}, u32[]{:S(2)}, u32[]{:S(2)}) collective-permute-start(f32[80,224]{1,0:T(8,128)S(1)} %dynamic-slice_add_fusion.1), channel_id=1, source_target_pairs={{0,16},{8,24},{16,32},{24,40},{32,48},{40,56},{48,64},{56,72},{64,... | collective-permute-start | bytes 215048 | tf_op jit(solution)/shard_map/ppermute | solution.py:278
  58.6 9.8 %collective-permute-start.39 = (f32[80,224]{1,0:T(8,128)S(1)}, f32[80,224]{1,0:T(8,128)S(1)}, u32[]{:S(2)}, u32[]{:S(2)}) collective-permute-start(f32[80,224]{1,0:T(8,128)S(1)} %get-tuple-element.284), channel_id=1, source_target_pairs={{0,48},{8,56},{16,64},{24,72},{32,80},{40,88},{48,96},{56,104},{64... | collective-permute-start | bytes 215048 | tf_op jit(solution)/shard_map/ppermute | solution.py:278
  58.7 9.8 %collective-permute-start.38 = (f32[80,224]{1,0:T(8,128)S(1)}, f32[80,224]{1,0:T(8,128)S(1)}, u32[]{:S(2)}, u32[]{:S(2)}) collective-permute-start(f32[80,224]{1,0:T(8,128)S(1)} %get-tuple-element.283), channel_id=1, source_target_pairs={{0,80},{8,88},{16,96},{24,104},{32,112},{40,120},{48,0},{56,8},{64... | collective-permute-start | bytes 215048 | tf_op jit(solution)/shard_map/ppermute | solution.py:278
  63.7 12.6 %collective-permute-start.30 = (bf16[224,640]{1,0:T(8,128)(2,1)}, bf16[224,640]{1,0:T(8,128)(2,1)}, u32[]{:S(2)}, u32[]{:S(2)}) collective-permute-start(bf16[224,640]{1,0:T(8,128)(2,1)} %copy-done.4), channel_id=1, source_target_pairs={{0,4},{1,5},{2,6},{3,7},{4,0},{5,1},{6,2},{7,3},{8,12},{9,13},{10,... | collective-permute-start | bytes 860168 | tf_op jit(solution)/shard_map/ppermute | solution.py:268
  65.2 13.4 %collective-permute-start.29 = (bf16[224,640]{1,0:T(8,128)(2,1)}, bf16[224,640]{1,0:T(8,128)(2,1)}, u32[]{:S(2)}, u32[]{:S(2)}) collective-permute-start(bf16[224,640]{1,0:T(8,128)(2,1)} %copy-done.4), channel_id=1, source_target_pairs={{0,3},{1,0},{2,1},{3,2},{4,7},{5,4},{6,5},{7,6},{8,11},{9,8},{10,9... | collective-permute-start | bytes 860168 | tf_op jit(solution)/shard_map/ppermute | solution.py:268
  65.2 13.7 %collective-permute-start.28 = (bf16[224,640]{1,0:T(8,128)(2,1)}, bf16[224,640]{1,0:T(8,128)(2,1)}, u32[]{:S(2)}, u32[]{:S(2)}) collective-permute-start(bf16[224,640]{1,0:T(8,128)(2,1)} %copy-done.4), channel_id=1, source_target_pairs={{0,1},{1,2},{2,3},{3,0},{4,5},{5,6},{6,7},{7,4},{8,9},{9,10},{10,1... | collective-permute-start | bytes 860168 | tf_op jit(solution)/shard_map/ppermute | solution.py:268
  68.5 6.3 %collective-permute-start.40 = (f32[80,224]{1,0:T(8,128)S(1)}, f32[80,224]{1,0:T(8,128)S(1)}, u32[]{:S(2)}, u32[]{:S(2)}) collective-permute-start(f32[80,224]{1,0:T(8,128)S(1)} %add_add_fusion.2), channel_id=1, source_target_pairs={{0,128},{8,136},{16,144},{24,152},{32,160},{40,168},{48,176},{56,1... | collective-permute-start | bytes 215048 | tf_op jit(solution)/shard_map/ppermute | solution.py:278
  74.8 5.9 %collective-permute-start.41 = (f32[80,224]{1,0:T(8,128)S(1)}, f32[80,224]{1,0:T(8,128)}, u32[]{:S(2)}, u32[]{:S(2)}) collective-permute-start(f32[80,224]{1,0:T(8,128)S(1)} %add.572), channel_id=1, source_target_pairs={{0,8},{8,0},{16,24},{24,16},{32,40},{40,32},{48,56},{56,48},{64,72... | collective-permute-start | bytes 215048 | tf_op jit(solution)/shard_map/ppermute | solution.py:278
  75.0 18.6 %copy-start.5 = (bf16[224,640]{1,0:T(8,128)(2,1)S(1)}, bf16[224,640]{1,0:T(8,128)(2,1)}, u32[]{:S(2)}) copy-start(bf16[224,640]{1,0:T(8,128)(2,1)} %copy-done.4) | copy-start | bytes 860164
  75.0 11.7 %collective-permute-start.31 = (bf16[224,640]{1,0:T(8,128)(2,1)}, bf16[224,640]{1,0:T(8,128)(2,1)S(1)}, u32[]{:S(2)}, u32[]{:S(2)}) collective-permute-start(bf16[224,640]{1,0:T(8,128)(2,1)} %copy-done.4), channel_id=1, source_target_pairs={{0,2},{1,3},{2,0},{3,1},{4,6},{5,7},{6,4},{7,5},{8,10},{9,11},{10,... | collective-permute-start | bytes 860168 | tf_op jit(solution)/shard_map/ppermute | solution.py:268
  76.3 15.8 %collective-permute-start.34 = (bf16[224,640]{1,0:T(8,128)(2,1)}, bf16[224,640]{1,0:T(8,128)(2,1)S(1)}, u32[]{:S(2)}, u32[]{:S(2)}) collective-permute-start(bf16[224,640]{1,0:T(8,128)(2,1)} %collective-permute-done.30.refs_3_), channel_id=1, source_target_pairs={{0,2},{1,3},{2,0},{3,1},{4,6},{5,7},{6,4},{7,5},{8,10},{9,11},{10,... | collective-permute-start | bytes 860168 | tf_op jit(solution)/shard_map/ppermute | solution.py:268
  78.7 13.5 %collective-permute-start.33 = (bf16[224,640]{1,0:T(8,128)(2,1)}, bf16[224,640]{1,0:T(8,128)(2,1)S(1)}, u32[]{:S(2)}, u32[]{:S(2)}) collective-permute-start(bf16[224,640]{1,0:T(8,128)(2,1)} %collective-permute-done.29.refs_2_), channel_id=1, source_target_pairs={{0,4},{1,5},{2,6},{3,7},{4,0},{5,1},{6,2},{7,3},{8,12},{9,13},{10,... | collective-permute-start | bytes 860168 | tf_op jit(solution)/shard_map/ppermute | solution.py:268
  78.9 14.7 %collective-permute-start.32 = (bf16[224,640]{1,0:T(8,128)(2,1)}, bf16[224,640]{1,0:T(8,128)(2,1)S(1)}, u32[]{:S(2)}, u32[]{:S(2)}) collective-permute-start(bf16[224,640]{1,0:T(8,128)(2,1)} %collective-permute-done.28.refs_1_), channel_id=1, source_target_pairs={{0,4},{1,5},{2,6},{3,7},{4,0},{5,1},{6,2},{7,3},{8,12},{9,13},{10,... | collective-permute-start | bytes 860168 | tf_op jit(solution)/shard_map/ppermute | solution.py:268
  93.6 9.9 %copy-start.24 = (bf16[256,128]{1,0:T(8,128)(2,1)S(1)}, bf16[256,128]{1,0:T(8,128)(2,1)}, u32[]{:S(2)}) copy-start(bf16[256,128]{1,0:T(8,128)(2,1)} %constant.540.clone..sunk.2) | copy-start | bytes 196612
  93.6 9.9 %copy-start.26 = (s32[1024]{0:T(1024)S(1)}, s32[1024]{0:T(1024)}, u32[]{:S(2)}) copy-start(s32[1024]{0:T(1024)} %param.13) | copy-start | bytes 12292
  93.7 9.9 %copy-start.27 = (bf16[2,64,224]{2,1,0:T(8,128)(2,1)S(1)}, bf16[2,64,224]{2,1,0:T(8,128)(2,1)}, u32[]{:S(2)}) copy-start(bf16[2,64,224]{2,1,0:T(8,128)(2,1)} %constant.543.clone..sunk.2) | copy-start | bytes 172036

commit v2 on v0

v2 whole, which is shorter than its diff:
```python
import functools

import jax
import jax.numpy as jnp
import ml_dtypes
import numpy as np
from jax import lax
from jax.experimental import pallas as pl
from jax.experimental.pallas import tpu as pltpu
from jax.sharding import PartitionSpec as P

TILE, BAND = 64, 8
DECAY = 0.9
TOK, DW = 1024, 1792
ROWS, COLS = 1216, 224
CHUNK = 256
NB = DW // CHUNK
NA = -(-ROWS // CHUNK)
BROWS = NA * 32
BCOLS = DW // TILE * BAND
LIVE = 640
FLAG_ROW = BROWS - 1
BIG = [slice(0, 512), slice(512, 1024), slice(1024, ROWS)]
SMALL = [slice(a * CHUNK, min(a * CHUNK + CHUNK, ROWS)) for a in range(NA)]
F32, BF16 = jnp.float32, jnp.bfloat16
MIB = 1 << 20
VMEM_MIB = 20


def _basis():
    k = np.arange(BAND)[:, None]
    n = np.arange(TILE)[None]
    scale = np.where(k == 0, np.sqrt(1.0 / TILE), np.sqrt(2.0 / TILE))
    return (scale * np.cos(np.pi * (2 * n + 1) * k / (2 * TILE))).astype(np.float32)


def _split(a):
    hi = a.astype(ml_dtypes.bfloat16)
    lo = (a - hi.astype(np.float32)).astype(ml_dtypes.bfloat16)
    return hi, lo


def _constants():
    d = _basis()
    block = np.kron(np.eye(4, dtype=np.float32), d)
    hi, lo = _split(block)
    rows_down = np.concatenate([hi, lo], 0)
    rows_up = np.concatenate([hi, hi, lo, lo], 0).T.copy()
    cols_down = np.concatenate([np.kron(np.eye(4, dtype=np.float32)[q : q + 1], rows_down.astype(np.float32).T) for q in range(4)], 0)
    merge = np.zeros((512, BCOLS), np.float32)
    for i in range(BCOLS):
        merge[i // 32 * 64 + i % 32, i] = merge[i // 32 * 64 + 32 + i % 32, i] = 1
    seven = np.kron(np.eye(7, dtype=np.float32), d)
    local = []
    for odd in range(2):
        part = seven[24 * odd : 24 * odd + 32, COLS * odd : COLS * odd + COLS]
        local.append(np.concatenate(_split(part), 0))
    return dict(
        rows_down=rows_down,
        rows_up=rows_up,
        cols_down=cols_down.astype(ml_dtypes.bfloat16),
        merge=merge.astype(ml_dtypes.bfloat16),
        local=np.stack(local),
    )


CONST = _constants()


def _dot(a, b, ca=1, cb=0):
    return lax.dot_general(a, b, (((ca,), (cb,)), ((), ())), preferred_element_type=F32)


def _halves(x):
    hi = x.astype(BF16)
    return hi, (x - hi.astype(F32)).astype(BF16)


def _place_live(mask, live):
    ones = (mask == 1).astype(F32)
    at = lax.broadcasted_iota(jnp.int32, (128, 128), 0)
    to = lax.broadcasted_iota(jnp.int32, (128, 128), 1)
    upto = _dot(ones.astype(BF16), (at <= to).astype(BF16))
    slot = lax.broadcasted_iota(jnp.int32, (live, 128), 0).astype(F32)
    before = jnp.zeros((1, 1), F32)
    parts = []
    for s in range(TOK // 128):
        place = upto[s : s + 1, :] + before - 1.0
        place = jnp.where(ones[s : s + 1, :] > 0.5, place, -1.0)
        parts.append(jnp.where(slot == place, 1.0, 0.0).astype(BF16))
        before = before + upto[s : s + 1, 127:128]
    return jnp.concatenate(parts, 1), before


def _expand_setup(band, down, stack):
    b_hi, b_lo = _halves(band)
    for b in range(NB):
        at = slice(32 * b, 32 * b + 32)
        wide = _dot(b_hi[:, at], down[:32]) + _dot(b_lo[:, at], down[:32]) + _dot(b_hi[:, at], down[32:])
        hi, lo = _halves(wide)
        for a in range(NA):
            for q, part in enumerate((hi, lo, hi, lo)):
                stack[a, 32 * q : 32 * q + 32, CHUNK * b : CHUNK * b + CHUNK] = part[32 * a : 32 * a + 32, :]


def _fetch(sems, *pairs):
    copies = [pltpu.make_async_copy(src, dst, sems.at[i]) for i, (src, dst) in enumerate(pairs)]
    for c in copies:
        c.start()
    return copies


def _wait(copies):
    for c in copies:
        c.wait()


def _rows(src, dst, cuts, sems):
    return [pltpu.make_async_copy(src.at[r, :], dst.at[r, :], sems.at[i]) for i, r in enumerate(cuts)]


def _weights_kernel(live, parity, mask, cot, local, out_w, out_p, out_n, mask_v, cot_v, local_v, w_v, p_v, n_v, sems, out_sems):
    copies = _fetch(sems, (mask, mask_v), (cot, cot_v), (local.at[parity[0]], local_v))
    copies[0].wait()
    onehot, count = _place_live(mask_v[...], live)
    _wait(copies[1:])
    picked = _dot(cot_v[...], onehot, 1, 1).astype(BF16)
    both = _dot(local_v[...], picked)
    w_v[...] = picked
    p_v[...] = both[:32] + both[32:]
    n_v[...] = jnp.broadcast_to(count, (8, 128))
    _wait(_fetch(out_sems, (w_v, out_w), (p_v, out_p), (n_v, out_n)))


def _local_kernel(live, mask, cols_down, rows_down, merge, hid, mom, out_h, out_p, out_m, *refs):
    mask_v, cols_v, rows_v, merge_v, hid_v, cols, wide, sems = refs
    copies = _fetch(sems, (mask, mask_v), (rows_down, rows_v), (hid, hid_v), (cols_down, cols_v), (merge, merge_v))
    _wait(copies[:2])
    down = rows_v[...]
    onehot = _place_live(mask_v[...], live)[0]
    copies[2].wait()
    for r in BIG:
        out_h[r, :] = _dot(hid_v[r, :], onehot, 1, 1).astype(BF16)
    for a, r in enumerate(SMALL):
        both = _dot(down[:, : r.stop - r.start], out_h[r, :])
        hi, lo = _halves(both[:32] + both[32:])
        out_p[32 * a : 32 * a + 32, :] = hi
        out_p[BROWS + 32 * a : BROWS + 32 * a + 32, :] = lo
    _wait(copies[3:])
    for r in BIG:
        cols[r, :256] = _dot(mom[r, :1024], cols_v[...])
        cols[r, 256:] = _dot(mom[r, 1024:], cols_v[:768, :])
    for a, r in enumerate(SMALL):
        n = r.stop - r.start
        hi, lo = _halves(cols[r, :])
        both = _dot(down[:, :n], hi)
        wide[32 * a : 32 * a + 32, :] = both[:32] + both[32:] + _dot(down[:32, :n], lo)
    hi, lo = _halves(wide[...])
    out_m[...] = _dot(hi, merge_v[...]) + _dot(lo, merge_v[...])


def _band_kernel(live, places, parities, hid_p, mom_band, count, local, *refs):
    shards, out, own_across, up_down, local_v, cot_p, sems = refs[:9], *refs[9:]
    whole = [up_down.at[0], up_down.at[1], own_across.at[1], own_across.at[0]]
    copies = _fetch(sems, (local, local_v))
    cot_p[...] = jnp.zeros_like(cot_p)
    for s in range(4):
        whole[s][...] = shards[s][...]
    _wait(copies)
    for s in range(8):
        at = pl.ds(pl.multiple_of(places[s], 8), 32)
        if s < 3:
            both = _dot(local_v[parities[s]], shards[s][...])
            cot_p[at, :] += both[:32] + both[32:]
        else:
            cot_p[at, :] += shards[s + 1][...]
    h_hi, h_lo = hid_p[:BROWS, :], hid_p[BROWS:, :]
    w_hi, w_lo = _halves(cot_p[...])
    grad = _dot(h_hi, w_hi, 1, 1) + _dot(h_lo, w_hi, 1, 1) + _dot(h_hi, w_lo, 1, 1)
    band = DECAY * mom_band[...] + grad
    row = lax.broadcasted_iota(jnp.int32, band.shape, 0)
    over = jnp.where(count[0:1, 0:1] > live + 0.5, 1.0, 0.0)
    out[...] = jnp.where(row == FLAG_ROW, over, band)


def _momentum_kernel(live, places, band, rows_down, rows_up, mom, hid, *refs):
    pairs, out, rows_v, up_v, cot, out_v, stack, sems, out_sems = refs[:4], *refs[4:]
    copies = _fetch(sems, (rows_down, rows_v), (rows_up, up_v))
    stores = _rows(out_v, out, SMALL, out_sems)
    for s in range(8):
        cot[pl.ds(pl.multiple_of(places[s], 16), COLS), :] = pairs[s // 2][s % 2]
    _wait(copies)
    _expand_setup(band[...], rows_v[...], stack)
    for a, r in enumerate(SMALL):
        for b in range(NB):
            w = slice(CHUNK * b, CHUNK * b + CHUNK)
            kept = _dot(hid[r, :], cot[w, :], 1, 1) - _dot(up_v[: r.stop - r.start, :], stack[a, :, w])
            out_v[r, w] = (DECAY * mom[r, w].astype(F32) + kept).astype(BF16)
        stores[a].start()
    _wait(stores)


def _update_kernel(core, mine, back, rows_down, rows_up, out, over, rows_v, up_v, out_v, stack, sems, out_sems):
    copies = _fetch(sems, (rows_down, rows_v), (rows_up, up_v))
    stores = _rows(out_v, out, SMALL, out_sems)
    first = core[0] == 0
    band = jnp.concatenate([jnp.where(first, mine[...], back[...]), jnp.where(first, back[...], mine[...])], 0)
    over[0] = jnp.max(band[FLAG_ROW:, :]).astype(jnp.int32)
    _wait(copies)
    _expand_setup(band, rows_v[...], stack)
    for a, r in enumerate(SMALL):
        out_v[r, :] = _dot(up_v[: r.stop - r.start, :], stack[a]).astype(BF16)
        stores[a].start()
    _wait(stores)


SM = pl.BlockSpec(memory_space=pltpu.SMEM)
VM = pl.BlockSpec(memory_space=pltpu.VMEM)
HB = pl.BlockSpec(memory_space=pltpu.HBM)


def _sems(*n):
    return pltpu.SemaphoreType.DMA(n)


def _struct(shape, dtype):
    return jax.ShapeDtypeStruct(shape, dtype)


def _call(kernel, us, ins, outs, scratch, *args, grant=VMEM_MIB):
    name = kernel.func.__name__ if isinstance(kernel, functools.partial) else kernel.__name__
    return pl.pallas_call(
        kernel,
        out_shape=[_struct(*o[1:]) for o in outs],
        in_specs=ins,
        out_specs=[o[0] for o in outs],
        scratch_shapes=scratch,
        compiler_params=pltpu.CompilerParams(vmem_limit_bytes=grant * MIB),
        cost_estimate=pl.CostEstimate(flops=int(us * 1e9), bytes_accessed=int(us * 3.3e6), transcendentals=0),
        name=name.strip("_"),
    )(*args)


V = pltpu.VMEM
MASK = V((8, 128), jnp.int32)
DOWN = V((64, CHUNK), BF16)
UP = V((CHUNK, 128), BF16)
STACK = V((NA, 128, DW), BF16)


def _weights(live, parity, mask, cot, local):
    return _call(
        functools.partial(_weights_kernel, live),
        2.5,
        [SM, HB, HB, HB],
        [(HB, (COLS, live), BF16), (HB, (32, live), F32), (HB, (8, 128), F32)],
        [MASK, V((COLS, TOK), BF16), V((64, COLS), BF16), V((COLS, live), BF16), V((32, live), F32), V((8, 128), F32), _sems(3), _sems(3)],
        parity, mask, cot, local,
    )


def _local(live, mask, cols_down, rows_down, merge, hid, mom):
    return _call(
        functools.partial(_local_kernel, live),
        6,
        [HB, HB, HB, HB, HB, VM],
        [(VM, (ROWS, live), BF16), (VM, (2 * BROWS, live), BF16), (VM, (BROWS, BCOLS), F32)],
        [MASK, V((1024, 256), BF16), DOWN, V((512, BCOLS), BF16), V((ROWS, TOK), BF16),
         V((ROWS, 512), F32), V((BROWS, 512), F32), _sems(5)],
        mask, cols_down, rows_down, merge, hid, mom,
    )


def _band(live, places, parities, hid_p, mom_band, count, local, shards):
    return _call(
        functools.partial(_band_kernel, live),
        3,
        [SM, SM, VM, VM, VM, HB] + [VM] * 9,
        [(VM, (BROWS, BCOLS), F32), (VM, (2, COLS, live), BF16), (VM, (2, COLS, live), BF16)],
        [V((2, 64, COLS), BF16), V((BCOLS, live), F32), _sems(1)],
        places, parities, hid_p, mom_band, count, local, *shards,
    )


def _momentum(live, places, band, rows_down, rows_up, mom, hid, pairs):
    return _call(
        functools.partial(_momentum_kernel, live),
        8,
        [SM, VM, HB, HB] + [VM] * 6,
        [(HB, (ROWS, DW), BF16)],
        [DOWN, UP, V((DW, live), BF16), V((ROWS, DW), BF16), STACK, _sems(2), _sems(NA)],
        places, band, rows_down, rows_up, mom, hid, *pairs,
    )[0]


def _update(core, mine, back, rows_down, rows_up):
    return _call(
        _update_kernel,
        3.5,
        [SM, VM, VM, HB, HB],
        [(HB, (ROWS, DW), BF16), (SM, (1,), jnp.int32)],
        [DOWN, UP, V((ROWS, DW), BF16), STACK, _sems(2), _sems(NA)],
        core, mine, back, rows_down, rows_up,
    )


def _tensor_shift(a, dx, dy):
    pairs = [(x * 4 + y, (x + dx) % 2 * 4 + (y + dy) % 4) for x in range(2) for y in range(4)]
    return lax.ppermute(a, "tensor", pairs)


def _replica_shift(a, df, dz, dc):
    pairs = [
        (f * 16 + z * 2 + c, (f + df) % 2 * 16 + (z + dz) % 8 * 2 + (c + dc) % 2)
        for f in range(2)
        for z in range(8)
        for c in range(2)
    ]
    return lax.ppermute(a, "replica", pairs)


SHIFTS = ((0, 1), (0, 3), (1, 0), (0, 0), (0, 2), (1, 2), (1, 1), (1, 3))


def _sum_planes(band, core):
    half = BROWS // 2
    mine = lax.dynamic_slice(band, (core * half, 0), (half, BCOLS))
    other = lax.dynamic_slice(band, ((1 - core) * half, 0), (half, BCOLS))
    one = mine + _replica_shift(other, 0, 0, 1)
    below, above = _replica_shift(one, 0, 1, 0), _replica_shift(one, 0, 7, 0)
    two, three = one + above, one + below + above
    return three, _replica_shift(three, 0, 5, 0), _replica_shift(two, 0, 3, 0)


def _step(live, hidden, out_grad, mask, mom):
    c = {k: jnp.asarray(v) for k, v in CONST.items()}
    index = lax.axis_index("tensor").astype(jnp.int32)
    core = (lax.axis_index("replica") % 2).astype(jnp.int32)
    x, y = index // 4, index % 4
    owners = [(x + dx) % 2 * 4 + (y - dy) % 4 for dx, dy in SHIFTS]
    places = jnp.stack([owners[s] * COLS for s in (3, 2, 4, 5, 0, 1, 6, 7)])
    band_places = jnp.stack([o // 2 * 56 + o % 2 * 24 for o in owners])

    parities = jnp.stack([o % 2 for o in owners])

    cot, cot_p, count = _weights(live, (index % 2).reshape(1), mask, out_grad, c["local"])
    far_p = [_tensor_shift(cot_p, *s) for s in SHIFTS[4:]]
    near = [_tensor_shift(cot, *s) for s in SHIFTS[:3]]
    hid, hid_p, mom_band = _local(live, mask, c["cols_down"], c["rows_down"], c["merge"], hidden, mom)
    band, own_across, up_down = _band(live, band_places, parities, hid_p, mom_band, count, c["local"], near + [cot, cot_p] + far_p)
    opposite, beside = _tensor_shift(own_across, 0, 2), _tensor_shift(up_down, 1, 0)
    sums = _sum_planes(band, core)
    *sums, opposite, beside = lax.optimization_barrier((*sums, opposite, beside))
    eight = sums[0] + sums[1] + sums[2]
    whole = eight + _replica_shift(eight, 1, 0, 0)
    pairs = [own_across, opposite, up_down, beside]
    momentum_out = _momentum(live, places, band, c["rows_down"], c["rows_up"], mom, hid, pairs)
    whole, momentum_out = lax.optimization_barrier((whole, momentum_out))
    back = _replica_shift(whole, 0, 0, 1)
    band_update, over = _update(core.reshape(1), whole, back, c["rows_down"], c["rows_up"])
    return momentum_out, band_update, over.reshape(())


def shards(hidden, out_grad, token_mask, momentum):
    mask = token_mask.reshape(8, 128)
    hidden, out_grad = hidden.T, out_grad.T
    mom = momentum[0]
    state = _step(LIVE, hidden, out_grad, mask, mom)
    momentum_out, band_update, _ = lax.while_loop(
        lambda s: s[2] > 0,
        lambda s: _step(TOK, hidden, out_grad, jnp.where(s[2] > 0, mask, 0), mom),
        state,
    )
    return momentum_out[None], band_update


def solution(mesh):
    placed = (P("replica", "tensor"), P("replica", "tensor"), P("replica"), P("replica", "tensor", None))
    return jax.shard_map(
        shards,
        mesh=mesh,
        in_specs=placed,
        out_specs=(P("replica", "tensor", None), P("tensor", None)),
        check_vma=False,
    )
```

time: 390 us -> 70.2 us (0.18)
  the two profiles are of different devices: /device:TPU:24 before, /device:TPU:73 now
where the time goes in v2:
time: 70.2 us; the launch traced here: 70 us
  starting transfers between devices  26.4 us (38%)
  Pallas kernels  21.7 us (31%)
  waiting for transfers between devices  14.7 us (21%)
  local copies, waits for them, and re-layouts  5.27 us (8%)
  between operations  1.05 us (1%)
  loops' own time  0.8 us (1%)
    pallas_call x5, Pallas kernels, _call(): pl.pallas_call(kernel, out_shape=[_struct(*o[1:]) for o in outs], in_spec...  21.7 us
    ppermute x7, starting transfers between devices, _replica_shift(): return lax.ppermute(a, 'replica', pairs)  13.3 us
    ppermute x9, starting transfers between devices, _tensor_shift(): return lax.ppermute(a, 'tensor', pairs)  13.1 us
    ppermute x7, waiting for transfers between devices, _replica_shift(): return lax.ppermute(a, 'replica', pairs)  12.6 us
    unnamed x34, local copies, waits for them, and re-layouts  5 us
    ppermute x9, waiting for transfers between devices, _tensor_shift(): return lax.ppermute(a, 'tensor', pairs)  2.06 us
  transfers between devices with their start and end apart: 16, of which 5 were waited for; matrix products, arithmetic and copies ran while one was open for 0% of the time, Pallas kernels for 20%

profile of v2, /device:TPU:73, one launch (start us, length us, event | category | flops | bytes accessed | tf_op | source)
XLA Modules:
  0.0 70.0 jit_solution(16654388901473257149)
XLA Ops:
  0.6 0.0 copy-start.13
  0.7 0.8 %copy-done.13 = bf16[2,64,224]{2,1,0:T(8,128)(2,1)S(1)} copy-done((bf16[2,64,224]{2,1,0:T(8,128)(2,1)S(1)}, bf16[2,64,224]{2,1,0:T(8,128)(2,1)}, u32[]{:S(2)}) %copy-start.13) | copy-done | bytes 57368
  1.5 0.0 copy-start.27
  1.5 0.0 copy-start.29
  1.5 2.2 %weights_kernel.6 = (bf16[224,640]{1,0:T(8,128)(2,1)S(1)}, f32[32,640]{1,0:T(8,128)S(1)}, f32[8,128]{1,0:T(8,128)S(1)}) custom-call(s32[1]{0:T(128)} %bitcast.19.parity, s32[8,128]{1,0:T(8,128)} %bitcast.113, bf16[224,1024]{1,0:T(8,128)(2,1)} %bitcast.20.cot, bf16[2,64,224]{2,1,0:T(8,128)(2,1)S(1)} %copy-done.13), custom_call_target="tpu_custom_call" | custom-call | flops 2500000000 | bytes 8250000 | tf_op jit(solution)/shard_map/weights_kernel/pallas_call | solution.py:232
  3.7 1.2 %collective-permute-start.22 = (f32[32,640]{1,0:T(8,128)S(1)}, f32[32,640]{1,0:T(8,128)S(1)}, u32[]{:S(2)}, u32[]{:S(2)}) collective-permute-start(f32[32,640]{1,0:T(8,128)S(1)} %get-tuple-element.242.refs_4_), channel_id=1, source_target_pairs={{0,7},{1,4},{2,5},{3,6},{4,3},{5,0},{6,1},{7,2},{8,15},{9,12},{10,... | collective-permute-start | bytes 245768 | tf_op jit(solution)/shard_map/ppermute | solution.py:309
  4.9 1.3 %collective-permute-start.21 = (f32[32,640]{1,0:T(8,128)S(1)}, f32[32,640]{1,0:T(8,128)S(1)}, u32[]{:S(2)}, u32[]{:S(2)}) collective-permute-start(f32[32,640]{1,0:T(8,128)S(1)} %get-tuple-element.242.refs_4_), channel_id=1, source_target_pairs={{0,5},{1,6},{2,7},{3,4},{4,1},{5,2},{6,3},{7,0},{8,13},{9,14},{10,... | collective-permute-start | bytes 245768 | tf_op jit(solution)/shard_map/ppermute | solution.py:309
  6.2 4.2 %collective-permute-start.20 = (f32[32,640]{1,0:T(8,128)S(1)}, f32[32,640]{1,0:T(8,128)S(1)}, u32[]{:S(2)}, u32[]{:S(2)}) collective-permute-start(f32[32,640]{1,0:T(8,128)S(1)} %get-tuple-element.242.refs_4_), channel_id=1, source_target_pairs={{0,6},{1,7},{2,4},{3,5},{4,2},{5,3},{6,0},{7,1},{8,14},{9,15},{10,... | collective-permute-start | bytes 245768 | tf_op jit(solution)/shard_map/ppermute | solution.py:309
  10.3 0.0 collective-permute-start.19
  10.3 0.3 collective-permute-start.18
  10.6 1.2 %collective-permute-start.17 = (bf16[224,640]{1,0:T(8,128)(2,1)S(1)}, bf16[224,640]{1,0:T(8,128)(2,1)S(1)}, u32[]{:S(2)}, u32[]{:S(2)}) collective-permute-start(bf16[224,640]{1,0:T(8,128)(2,1)S(1)} %get-tuple-element.241.refs_3_), channel_id=1, source_target_pairs={{0,3},{1,0},{2,1},{3,2},{4,7},{5,4},{6,5},{7,6},{8,11},{9,8},{10,9... | collective-permute-start | bytes 860168 | tf_op jit(solution)/shard_map/ppermute | solution.py:309
  11.8 0.0 collective-permute-done.21.refs_7_
  11.8 0.3 collective-permute-start.16
  12.1 0.0 copy-start.14
  12.1 5.1 %local_kernel.6 = (bf16[1216,640]{1,0:T(8,128)(2,1)S(1)}, bf16[320,640]{1,0:T(8,128)(2,1)S(1)}, f32[160,224]{1,0:T(8,128)S(1)}) custom-call(s32[8,128]{1,0:T(8,128)S(1)} %bitcast.114, bf16[1024,256]{1,0:T(8,128)(2,1)S(1)} %copy-done.10, bf16[64,256]{1,0:T(8,128)(2,1)S(1)} %copy-done.15, bf16[512,224]{1,0:T(8,128)(2,1)S(1)} %copy-done.11, ...), custom_call_target="tpu_custom_call" | custom-call | flops 6000000000 | bytes 19800000 | tf_op jit(solution)/shard_map/local_kernel/pallas_call | solution.py:232
  17.3 0.0 copy-start.20
  17.3 1.1 %copy-done.20 = bf16[1216,640]{1,0:T(8,128)(2,1)} copy-done((bf16[1216,640]{1,0:T(8,128)(2,1)}, bf16[1216,640]{1,0:T(8,128)(2,1)S(1)}, u32[]{:S(2)}) %copy-start.20) | copy-done | bytes 1556504
  18.4 0.7 copy-done.24
  19.1 0.1 stack.266.places
  19.2 0.1 stack.275.parities
  19.3 0.0 collective-permute-done.20.refs_6_
  19.3 0.0 collective-permute-done.18.refs_2_
  19.3 2.0 %collective-permute-done.17.refs_1_ = bf16[224,640]{1,0:T(8,128)(2,1)S(1)} collective-permute-done((bf16[224,640]{1,0:T(8,128)(2,1)S(1)}, bf16[224,640]{1,0:T(8,128)(2,1)S(1)}, u32[]{:S(2)}, u32[]{:S(2)}) %collective-permute-start.17) | collective-permute-done | bytes 286752 | tf_op jit(solution)/shard_map/ppermute | solution.py:309
  21.3 0.0 collective-permute-done.16.refs_0_
  21.3 0.9 %copy-done.25 = f32[160,224]{1,0:T(8,128)S(1)} copy-done((f32[160,224]{1,0:T(8,128)S(1)}, f32[160,224]{1,0:T(8,128)}, u32[]{:S(2)}) %copy-start.25) | copy-done | bytes 143384
  22.2 1.7 %band_kernel.6 = (f32[160,224]{1,0:T(8,128)S(1)}, bf16[2,224,640]{2,1,0:T(8,128)(2,1)S(1)}, bf16[2,224,640]{2,1,0:T(8,128)(2,1)S(1)}) custom-call(s32[8]{0:T(128)S(1)} %stack.266.places, s32[8]{0:T(128)S(1)} %stack.275.parities, bf16[320,640]{1,0:T(8,128)(2,1)S(1)} %get-tuple-element.238.hid_p, f32[160,224]{1,0:T(8,128)S(1)} %copy-done.25, ...), custom_call_target="tpu_custom_call" | custom-call | flops 3000000000 | bytes 9900000 | tf_op jit(solution)/shard_map/band_kernel/pallas_call | solution.py:232
  23.9 1.4 %collective-permute-start.23 = (f32[80,224]{1,0:T(8,128)S(1)}, f32[80,224]{1,0:T(8,128)S(1)}, u32[]{:S(2)}, u32[]{:S(2)}) collective-permute-start(f32[80,224]{1,0:T(8,128)S(1)} %constant_dynamic-slice_fusion.1), channel_id=1, source_target_pairs={{0,8},{8,0},{16,24},{24,16},{32,40},{40,32},{48,56},{56,48},{64,72... | collective-permute-start | bytes 215048 | tf_op jit(solution)/shard_map/ppermute | solution.py:319
  25.3 3.5 %collective-permute-start.28 = (bf16[2,224,640]{2,1,0:T(8,128)(2,1)S(1)}, bf16[2,224,640]{2,1,0:T(8,128)(2,1)S(1)}, u32[]{:S(2)}, u32[]{:S(2)}) collective-permute-start(bf16[2,224,640]{2,1,0:T(8,128)(2,1)S(1)} %get-tuple-element.244.refs_0_), channel_id=1, source_target_pairs={{0,2},{1,3},{2,0},{3,1},{4,6},{5,7},{6,4},{7,5},{8,10},{9,11},{10,... | collective-permute-start | bytes 1720328 | tf_op jit(solution)/shard_map/ppermute | solution.py:309
  28.8 1.2 %collective-permute-start.29 = (bf16[2,224,640]{2,1,0:T(8,128)(2,1)S(1)}, bf16[2,224,640]{2,1,0:T(8,128)(2,1)S(1)}, u32[]{:S(2)}, u32[]{:S(2)}) collective-permute-start(bf16[2,224,640]{2,1,0:T(8,128)(2,1)S(1)} %get-tuple-element.245.refs_2_), channel_id=1, source_target_pairs={{0,4},{1,5},{2,6},{3,7},{4,0},{5,1},{6,2},{7,3},{8,12},{9,13},{10,... | collective-permute-start | bytes 1720328 | tf_op jit(solution)/shard_map/ppermute | solution.py:309
  30.0 0.0 collective-permute-done.23
  30.1 0.4 collective-permute-start.25
  30.4 1.7 %collective-permute-start.24 = (f32[80,224]{1,0:T(8,128)S(1)}, f32[80,224]{1,0:T(8,128)S(1)}, u32[]{:S(2)}, u32[]{:S(2)}) collective-permute-start(f32[80,224]{1,0:T(8,128)S(1)} %dynamic-slice_add_fusion.1), channel_id=1, source_target_pairs={{0,16},{8,24},{16,32},{24,40},{32,48},{40,56},{48,64},{56,72},{64,... | collective-permute-start | bytes 215048 | tf_op jit(solution)/shard_map/ppermute | solution.py:319
  32.2 2.0 %collective-permute-done.25 = f32[80,224]{1,0:T(8,128)S(1)} collective-permute-done((f32[80,224]{1,0:T(8,128)S(1)}, f32[80,224]{1,0:T(8,128)S(1)}, u32[]{:S(2)}, u32[]{:S(2)}) %collective-permute-start.25) | collective-permute-done | bytes 71712 | tf_op jit(solution)/shard_map/ppermute | solution.py:319
  34.2 5.3 %collective-permute-start.27 = (f32[80,224]{1,0:T(8,128)S(1)}, f32[80,224]{1,0:T(8,128)S(1)}, u32[]{:S(2)}, u32[]{:S(2)}) collective-permute-start(f32[80,224]{1,0:T(8,128)S(1)} %get-tuple-element.338), channel_id=1, source_target_pairs={{0,48},{8,56},{16,64},{24,72},{32,80},{40,88},{48,96},{56,104},{64... | collective-permute-start | bytes 215048 | tf_op jit(solution)/shard_map/ppermute | solution.py:319
  39.5 0.4 collective-permute-start.26
  39.9 0.1 stack.284.places
  40.0 2.0 %collective-permute-done.27 = f32[80,224]{1,0:T(8,128)S(1)} collective-permute-done((f32[80,224]{1,0:T(8,128)S(1)}, f32[80,224]{1,0:T(8,128)S(1)}, u32[]{:S(2)}, u32[]{:S(2)}) %collective-permute-start.27) | collective-permute-done | bytes 71712 | tf_op jit(solution)/shard_map/ppermute | solution.py:319
  42.0 7.7 %collective-permute-done.26 = f32[80,224]{1,0:T(8,128)S(1)} collective-permute-done((f32[80,224]{1,0:T(8,128)S(1)}, f32[80,224]{1,0:T(8,128)S(1)}, u32[]{:S(2)}, u32[]{:S(2)}) %collective-permute-start.26) | collective-permute-done | bytes 71712 | tf_op jit(solution)/shard_map/ppermute | solution.py:319
  49.7 0.0 collective-permute-done.28.refs_1_
  49.7 0.0 collective-permute-done.29.refs_3_
  49.7 2.6 %collective-permute-start.30 = (f32[80,224]{1,0:T(8,128)S(1)}, f32[80,224]{1,0:T(8,128)S(1)}, u32[]{:S(2)}, u32[]{:S(2)}) collective-permute-start(f32[80,224]{1,0:T(8,128)S(1)} %add_add_fusion.2), channel_id=1, source_target_pairs={{0,128},{8,136},{16,144},{24,152},{32,160},{40,168},{48,176},{56,1... | collective-permute-start | bytes 215048 | tf_op jit(solution)/shard_map/ppermute | solution.py:319
  52.3 1.4 %copy-done.21 = bf16[1216,640]{1,0:T(8,128)(2,1)S(1)} copy-done((bf16[1216,640]{1,0:T(8,128)(2,1)S(1)}, bf16[1216,640]{1,0:T(8,128)(2,1)}, u32[]{:S(2)}) %copy-start.21) | copy-done | bytes 1556504
  53.7 9.0 %momentum_kernel.6 = bf16[1216,1792]{1,0:T(8,128)(2,1)} custom-call(s32[8]{0:T(128)S(1)} %stack.284.places, f32[160,224]{1,0:T(8,128)S(1)} %get-tuple-element.243.band, bf16[64,256]{1,0:T(8,128)(2,1)S(1)} %copy-done.15, bf16[256,128]{1,0:T(8,128)(2,1)S(1)} %copy-done.12, bf16[1216,1792]{1,0:T(8,128)(2,1)} %bitcast.116, bf16[1216,640]{1,0:T(8,128)(2,1)S(1)} %copy-done.21, ...), custom_call_target="tpu_custom_call" | custom-call | flops 8000000000 | bytes 26400000 | tf_op jit(solution)/shard_map/momentum_kernel/pallas_call | solution.py:232
  62.7 0.0 collective-permute-done.30
  62.7 1.6 %collective-permute-start.31 = (f32[80,224]{1,0:T(8,128)S(1)}, f32[80,224]{1,0:T(8,128)S(1)}, u32[]{:S(2)}, u32[]{:S(2)}) collective-permute-start(f32[80,224]{1,0:T(8,128)S(1)} %add.588.mine), channel_id=1, source_target_pairs={{0,8},{8,0},{16,24},{24,16},{32,40},{40,32},{48,56},{56,48},{64,72... | collective-permute-start | bytes 215048 | tf_op jit(solution)/shard_map/ppermute | solution.py:319
  64.3 0.9 %collective-permute-done.31.back = f32[80,224]{1,0:T(8,128)S(1)} collective-permute-done((f32[80,224]{1,0:T(8,128)S(1)}, f32[80,224]{1,0:T(8,128)S(1)}, u32[]{:S(2)}, u32[]{:S(2)}) %collective-permute-start.31) | collective-permute-done | bytes 71712 | tf_op jit(solution)/shard_map/ppermute | solution.py:319
  65.2 3.7 %update_kernel.6 = (bf16[1216,1792]{1,0:T(8,128)(2,1)}, s32[1]{0:T(128)}) custom-call(s32[1]{0:T(128)} %bitcast.29.core, f32[80,224]{1,0:T(8,128)S(1)} %add.588.mine, f32[80,224]{1,0:T(8,128)S(1)} %collective-permute-done.31.back, bf16[64,256]{1,0:T(8,128)(2,1)S(1)} %copy-done.15, bf16[256,128]{1,0:T(8,128)(2,1)S(1)} %copy-done.12), custom_call_target="tpu_custom_call" | custom-call | flops 3500000000 | bytes 11550000 | tf_op jit(solution)/shard_map/update_kernel/pallas_call | solution.py:232
  69.0 0.8 %while.16 = (bf16[1216,1792]{1,0:T(8,128)(2,1)}, bf16[1216,1792]{1,0:T(8,128)(2,1)}, s32[]{:T(128)}, s32[8,128]{1,0:T(8,128)S(1)}, bf16[1216,1024]{1,0:T(8,128)(...) while((bf16[1216,1792]{1,0:T(8,128)(2,1)}, ...), condition=%wide.region_1.2_spmd.clone, body=%wide.region_0.1_spmd.sunk.clone.sunk | while | flops 23000127488 | bytes 159158256 | solution.py:369
  (32 shorter events, 0.1 us)
Async XLA Ops:
  0.6 0.8 %copy-start.13 = (bf16[2,64,224]{2,1,0:T(8,128)(2,1)S(1)}, bf16[2,64,224]{2,1,0:T(8,128)(2,1)}, u32[]{:S(2)}) copy-start(bf16[2,64,224]{2,1,0:T(8,128)(2,1)} %constant.575.clone.local) | copy-start | bytes 172036
  1.5 10.6 %copy-start.10 = (bf16[1024,256]{1,0:T(8,128)(2,1)S(1)}, bf16[1024,256]{1,0:T(8,128)(2,1)}, u32[]{:S(2)}) copy-start(bf16[1024,256]{1,0:T(8,128)(2,1)} %constant.573.clone.cols_down) | copy-start | bytes 1572868
  1.5 10.6 %copy-start.11 = (bf16[512,224]{1,0:T(8,128)(2,1)S(1)}, bf16[512,224]{1,0:T(8,128)(2,1)}, u32[]{:S(2)}) copy-start(bf16[512,224]{1,0:T(8,128)(2,1)} %constant.574.clone.merge) | copy-start | bytes 688132
  1.5 10.6 %copy-start.15 = (bf16[64,256]{1,0:T(8,128)(2,1)S(1)}, bf16[64,256]{1,0:T(8,128)(2,1)}, u32[]{:S(2)}) copy-start(bf16[64,256]{1,0:T(8,128)(2,1)} %constant.571.clone.rows_down) | copy-start | bytes 98308
  1.5 10.6 %copy-start.26 = (s32[1024]{0:T(1024)S(1)}, s32[1024]{0:T(1024)}, u32[]{:S(2)}) copy-start(s32[1024]{0:T(1024)} %param.13) | copy-start | bytes 12292
  1.5 10.6 %copy-start.27 = (bf16[1,1216,1792]{2,1,0:T(8,128)(2,1)S(1)}, bf16[1,1216,1792]{2,1,0:T(8,128)(2,1)}, u32[]{:S(2)}) copy-start(bf16[1,1216,1792]{2,1,0:T(8,128)(2,1)} %param.14) | copy-start | bytes 13074436
  1.5 10.6 %copy-start.29 = (bf16[1024,1216]{0,1:T(8,128)(2,1)S(1)}, bf16[1024,1216]{0,1:T(8,128)(2,1)}, u32[]{:S(2)}) copy-start(bf16[1024,1216]{0,1:T(8,128)(2,1)} %param.11) | copy-start | bytes 7471108
  3.7 6.9 %collective-permute-start.22 = (f32[32,640]{1,0:T(8,128)S(1)}, f32[32,640]{1,0:T(8,128)S(1)}, u32[]{:S(2)}, u32[]{:S(2)}) collective-permute-start(f32[32,640]{1,0:T(8,128)S(1)} %get-tuple-element.242.refs_4_), channel_id=1, source_target_pairs={{0,7},{1,4},{2,5},{3,6},{4,3},{5,0},{6,1},{7,2},{8,15},{9,12},{10,... | collective-permute-start | bytes 245768 | tf_op jit(solution)/shard_map/ppermute | solution.py:309
  4.9 6.9 %collective-permute-start.21 = (f32[32,640]{1,0:T(8,128)S(1)}, f32[32,640]{1,0:T(8,128)S(1)}, u32[]{:S(2)}, u32[]{:S(2)}) collective-permute-start(f32[32,640]{1,0:T(8,128)S(1)} %get-tuple-element.242.refs_4_), channel_id=1, source_target_pairs={{0,5},{1,6},{2,7},{3,4},{4,1},{5,2},{6,3},{7,0},{8,13},{9,14},{10,... | collective-permute-start | bytes 245768 | tf_op jit(solution)/shard_map/ppermute | solution.py:309
  6.2 13.1 %collective-permute-start.20 = (f32[32,640]{1,0:T(8,128)S(1)}, f32[32,640]{1,0:T(8,128)S(1)}, u32[]{:S(2)}, u32[]{:S(2)}) collective-permute-start(f32[32,640]{1,0:T(8,128)S(1)} %get-tuple-element.242.refs_4_), channel_id=1, source_target_pairs={{0,6},{1,7},{2,4},{3,5},{4,2},{5,3},{6,0},{7,1},{8,14},{9,15},{10,... | collective-permute-start | bytes 245768 | tf_op jit(solution)/shard_map/ppermute | solution.py:309
  10.3 8.9 %collective-permute-start.19 = (f32[32,640]{1,0:T(8,128)S(1)}, f32[32,640]{1,0:T(8,128)S(1)}, u32[]{:S(2)}, u32[]{:S(2)}) collective-permute-start(f32[32,640]{1,0:T(8,128)S(1)} %get-tuple-element.242.refs_4_), channel_id=1, source_target_pairs={{0,2},{1,3},{2,0},{3,1},{4,6},{5,7},{6,4},{7,5},{8,10},{9,11},{10,... | collective-permute-start | bytes 245768 | tf_op jit(solution)/shard_map/ppermute | solution.py:309
  10.3 9.0 %collective-permute-start.18 = (bf16[224,640]{1,0:T(8,128)(2,1)S(1)}, bf16[224,640]{1,0:T(8,128)(2,1)S(1)}, u32[]{:S(2)}, u32[]{:S(2)}) collective-permute-start(bf16[224,640]{1,0:T(8,128)(2,1)S(1)} %get-tuple-element.241.refs_3_), channel_id=1, source_target_pairs={{0,4},{1,5},{2,6},{3,7},{4,0},{5,1},{6,2},{7,3},{8,12},{9,13},{10,... | collective-permute-start | bytes 860168 | tf_op jit(solution)/shard_map/ppermute | solution.py:309
  10.6 10.7 %collective-permute-start.17 = (bf16[224,640]{1,0:T(8,128)(2,1)S(1)}, bf16[224,640]{1,0:T(8,128)(2,1)S(1)}, u32[]{:S(2)}, u32[]{:S(2)}) collective-permute-start(bf16[224,640]{1,0:T(8,128)(2,1)S(1)} %get-tuple-element.241.refs_3_), channel_id=1, source_target_pairs={{0,3},{1,0},{2,1},{3,2},{4,7},{5,4},{6,5},{7,6},{8,11},{9,8},{10,9... | collective-permute-start | bytes 860168 | tf_op jit(solution)/shard_map/ppermute | solution.py:309
  11.8 9.5 %collective-permute-start.16 = (bf16[224,640]{1,0:T(8,128)(2,1)S(1)}, bf16[224,640]{1,0:T(8,128)(2,1)S(1)}, u32[]{:S(2)}, u32[]{:S(2)}) collective-permute-start(bf16[224,640]{1,0:T(8,128)(2,1)S(1)} %get-tuple-element.241.refs_3_), channel_id=1, source_target_pairs={{0,1},{1,2},{2,3},{3,0},{4,5},{5,6},{6,7},{7,4},{8,9},{9,10},{10,1... | collective-permute-start | bytes 860168 | tf_op jit(solution)/shard_map/ppermute | solution.py:309
  12.1 9.2 %copy-start.14 = (bf16[2,64,224]{2,1,0:T(8,128)(2,1)S(1)}, bf16[2,64,224]{2,1,0:T(8,128)(2,1)}, u32[]{:S(2)}) copy-start(bf16[2,64,224]{2,1,0:T(8,128)(2,1)} %constant.575.clone.local) | copy-start | bytes 172036
  17.3 1.1 %copy-start.20 = (bf16[1216,640]{1,0:T(8,128)(2,1)}, bf16[1216,640]{1,0:T(8,128)(2,1)S(1)}, u32[]{:S(2)}) copy-start(bf16[1216,640]{1,0:T(8,128)(2,1)S(1)} %get-tuple-element.249.hid) | copy-start | bytes 4669444
  18.4 0.7 copy-start.24
  21.3 0.9 %copy-start.25 = (f32[160,224]{1,0:T(8,128)S(1)}, f32[160,224]{1,0:T(8,128)}, u32[]{:S(2)}) copy-start(f32[160,224]{1,0:T(8,128)} %copy-done.24) | copy-start | bytes 430084
  22.2 30.0 %copy-start.12 = (bf16[256,128]{1,0:T(8,128)(2,1)S(1)}, bf16[256,128]{1,0:T(8,128)(2,1)}, u32[]{:S(2)}) copy-start(bf16[256,128]{1,0:T(8,128)(2,1)} %constant.572.clone.rows_up) | copy-start | bytes 196612
  23.9 6.1 %collective-permute-start.23 = (f32[80,224]{1,0:T(8,128)S(1)}, f32[80,224]{1,0:T(8,128)S(1)}, u32[]{:S(2)}, u32[]{:S(2)}) collective-permute-start(f32[80,224]{1,0:T(8,128)S(1)} %constant_dynamic-slice_fusion.1), channel_id=1, source_target_pairs={{0,8},{8,0},{16,24},{24,16},{32,40},{40,32},{48,56},{56,48},{64,72... | collective-permute-start | bytes 215048 | tf_op jit(solution)/shard_map/ppermute | solution.py:319
  25.3 24.3 %collective-permute-start.28 = (bf16[2,224,640]{2,1,0:T(8,128)(2,1)S(1)}, bf16[2,224,640]{2,1,0:T(8,128)(2,1)S(1)}, u32[]{:S(2)}, u32[]{:S(2)}) collective-permute-start(bf16[2,224,640]{2,1,0:T(8,128)(2,1)S(1)} %get-tuple-element.244.refs_0_), channel_id=1, source_target_pairs={{0,2},{1,3},{2,0},{3,1},{4,6},{5,7},{6,4},{7,5},{8,10},{9,11},{10,... | collective-permute-start | bytes 1720328 | tf_op jit(solution)/shard_map/ppermute | solution.py:309
  28.8 20.9 %collective-permute-start.29 = (bf16[2,224,640]{2,1,0:T(8,128)(2,1)S(1)}, bf16[2,224,640]{2,1,0:T(8,128)(2,1)S(1)}, u32[]{:S(2)}, u32[]{:S(2)}) collective-permute-start(bf16[2,224,640]{2,1,0:T(8,128)(2,1)S(1)} %get-tuple-element.245.refs_2_), channel_id=1, source_target_pairs={{0,4},{1,5},{2,6},{3,7},{4,0},{5,1},{6,2},{7,3},{8,12},{9,13},{10,... | collective-permute-start | bytes 1720328 | tf_op jit(solution)/shard_map/ppermute | solution.py:309
  30.1 4.1 %collective-permute-start.25 = (f32[80,224]{1,0:T(8,128)S(1)}, f32[80,224]{1,0:T(8,128)S(1)}, u32[]{:S(2)}, u32[]{:S(2)}) collective-permute-start(f32[80,224]{1,0:T(8,128)S(1)} %dynamic-slice_add_fusion.1), channel_id=1, source_target_pairs={{0,112},{8,120},{16,0},{24,8},{32,16},{40,24},{48,32},{56,40},{64,... | collective-permute-start | bytes 215048 | tf_op jit(solution)/shard_map/ppermute | solution.py:319
  30.4 3.7 %collective-permute-start.24 = (f32[80,224]{1,0:T(8,128)S(1)}, f32[80,224]{1,0:T(8,128)S(1)}, u32[]{:S(2)}, u32[]{:S(2)}) collective-permute-start(f32[80,224]{1,0:T(8,128)S(1)} %dynamic-slice_add_fusion.1), channel_id=1, source_target_pairs={{0,16},{8,24},{16,32},{24,40},{32,48},{40,56},{48,64},{56,72},{64,... | collective-permute-start | bytes 215048 | tf_op jit(solution)/shard_map/ppermute | solution.py:319
  34.2 7.8 %collective-permute-start.27 = (f32[80,224]{1,0:T(8,128)S(1)}, f32[80,224]{1,0:T(8,128)S(1)}, u32[]{:S(2)}, u32[]{:S(2)}) collective-permute-start(f32[80,224]{1,0:T(8,128)S(1)} %get-tuple-element.338), channel_id=1, source_target_pairs={{0,48},{8,56},{16,64},{24,72},{32,80},{40,88},{48,96},{56,104},{64... | collective-permute-start | bytes 215048 | tf_op jit(solution)/shard_map/ppermute | solution.py:319
  39.5 10.2 %collective-permute-start.26 = (f32[80,224]{1,0:T(8,128)S(1)}, f32[80,224]{1,0:T(8,128)S(1)}, u32[]{:S(2)}, u32[]{:S(2)}) collective-permute-start(f32[80,224]{1,0:T(8,128)S(1)} %get-tuple-element.246), channel_id=1, source_target_pairs={{0,80},{8,88},{16,96},{24,104},{32,112},{40,120},{48,0},{56,8},{64... | collective-permute-start | bytes 215048 | tf_op jit(solution)/shard_map/ppermute | solution.py:319
  49.7 13.0 %collective-permute-start.30 = (f32[80,224]{1,0:T(8,128)S(1)}, f32[80,224]{1,0:T(8,128)S(1)}, u32[]{:S(2)}, u32[]{:S(2)}) collective-permute-start(f32[80,224]{1,0:T(8,128)S(1)} %add_add_fusion.2), channel_id=1, source_target_pairs={{0,128},{8,136},{16,144},{24,152},{32,160},{40,168},{48,176},{56,1... | collective-permute-start | bytes 215048 | tf_op jit(solution)/shard_map/ppermute | solution.py:319
  52.3 1.4 %copy-start.21 = (bf16[1216,640]{1,0:T(8,128)(2,1)S(1)}, bf16[1216,640]{1,0:T(8,128)(2,1)}, u32[]{:S(2)}) copy-start(bf16[1216,640]{1,0:T(8,128)(2,1)} %copy-done.20) | copy-start | bytes 4669444
  62.7 2.5 %collective-permute-start.31 = (f32[80,224]{1,0:T(8,128)S(1)}, f32[80,224]{1,0:T(8,128)S(1)}, u32[]{:S(2)}, u32[]{:S(2)}) collective-permute-start(f32[80,224]{1,0:T(8,128)S(1)} %add.588.mine), channel_id=1, source_target_pairs={{0,8},{8,0},{16,24},{24,16},{32,40},{40,32},{48,56},{56,48},{64,72... | collective-permute-start | bytes 215048 | tf_op jit(solution)/shard_map/ppermute | solution.py:319
  65.2 3.8 %copy-start.31 = (bf16[1024,256]{1,0:T(8,128)(2,1)S(1)}, bf16[1024,256]{1,0:T(8,128)(2,1)}, u32[]{:S(2)}) copy-start(bf16[1024,256]{1,0:T(8,128)(2,1)} %constant.573.clone..sunk.2) | copy-start | bytes 1572868
  65.2 3.8 %copy-start.33 = (bf16[512,224]{1,0:T(8,128)(2,1)S(1)}, bf16[512,224]{1,0:T(8,128)(2,1)}, u32[]{:S(2)}) copy-start(bf16[512,224]{1,0:T(8,128)(2,1)} %constant.574.clone..sunk.2) | copy-start | bytes 688132
  65.2 3.8 %copy-start.36 = (bf16[2,64,224]{2,1,0:T(8,128)(2,1)S(1)}, bf16[2,64,224]{2,1,0:T(8,128)(2,1)}, u32[]{:S(2)}) copy-start(bf16[2,64,224]{2,1,0:T(8,128)(2,1)} %constant.575.clone..sunk.2) | copy-start | bytes 172036
  65.2 3.8 %copy-start.38 = (bf16[64,256]{1,0:T(8,128)(2,1)S(1)}, bf16[64,256]{1,0:T(8,128)(2,1)}, u32[]{:S(2)}) copy-start(bf16[64,256]{1,0:T(8,128)(2,1)} %constant.571.clone..sunk.2) | copy-start | bytes 98308
